TPU v7x, 256 devices: a whole 4x4x8 slice. The times are simulated.
256 devices in a mesh: ctx: 64 (over x, z, core), tp: 4 (over y).
Axes of the slice: x: 4, y: 4, z: 8, core: 2. Of those that a mesh axis runs over, the one named last changes fastest.
Arguments:
- x_stream: bfloat16 [8192, 8192], P('ctx', 'tp'), may hold values from -6 to 6
- z_stream: bfloat16 [8192, 8192], P('ctx', 'tp'), may hold values from -6 to 6
- conv_kernel: float32 [4, 8192], P(None, 'tp'), may hold values from -3 to 3
- conv_bias: float32 [8192], P('tp'), may hold values from -0.5 to 0.5
- delta_down: bfloat16 [8192, 256], P('tp'), may hold values from -0.0625 to 0.0625
- state_proj: bfloat16 [32, 8192], P(None, 'tp'), may hold values from -0.0625 to 0.0625
- delta_up: bfloat16 [256, 8192], P(None, 'tp'), may hold values from -0.375 to 0.375
- delta_bias: float32 [8192], P('tp'), may hold values from -4.6 to -3
- log_decay: float32 [16, 8192], P(None, 'tp'), may hold values from -6 to 0
- skip_gain: float32 [8192], P('tp'), may hold values from 0.5 to 1.5
- queries: bfloat16 [8192, 4096], P('ctx', 'tp'), may hold values from -40 to 40
- key_heads: bfloat16 [8192, 1024], P('ctx', 'tp'), may hold values from -6 to 6
- values: bfloat16 [8192, 1024], P('ctx', 'tp'), may hold values from -24 to 24
- out_proj: bfloat16 [4096, 4096], P('tp', 'ctx'), may hold values from -0.09375 to 0.09375
- residual: bfloat16 [8192, 4096], P('ctx', 'tp'), may hold values from -1.5 to 1.5
Outputs:
- mixer_out: bfloat16 [8192, 8192], P('ctx', 'tp')
- block_out: bfloat16 [8192, 4096], P('ctx', 'tp')
All inputs are finite; a program needn't handle non-finite values.
Results may differ from a plain program's by a relative error of at most 0.02.
Values may be sent and summed in bfloat16 or wider, within the bound.
A program may use at most 192 MiB of HBM per device.

v0:
```python
import math

import jax
import jax.numpy as jnp
from jax import lax
from jax.sharding import PartitionSpec as P

NS = 16
CONV = 4
HD = 128


sub_len = 16
neg_fill = -1e30


def passed_along(value, axis, steps):
    count = lax.axis_size(axis)
    leading, last = (max(0, -steps), min(count, count - steps))
    return lax.ppermute(value, axis, [(source, source + steps) for source in range(leading, last)])


def prefix(value, axis, combine, identity):
    peers, here = (lax.axis_size(axis), lax.axis_index(axis))
    everything = jax.tree.map(lambda part: lax.all_gather(part, axis), value)
    start = jax.tree.map(
        lambda part, zero: jnp.broadcast_to(jnp.asarray(zero, part.dtype), part.shape),
        value,
        identity,
    )

    def lap(k, before):
        reached = k < here
        new = combine(before, jax.tree.map(lambda part: part[k], everything))
        return jax.tree.map(lambda a, b: jnp.where(reached, a, b), new, before)

    return lax.fori_loop(0, peers, lap, start)


def half_update(carried, query_half_rows, query_pos, key_piece, value_piece, first_row):
    running_max, running_sum, weighted = carried
    extent = key_piece.shape[0]
    kv_count = query_half_rows.shape[1]
    head_dim = query_half_rows.shape[3]

    def update():
        inverse_scale_factor = 1.0 / math.sqrt(head_dim)
        key_projected = key_piece.reshape(extent, kv_count, head_dim)
        value_projected = value_piece.reshape(extent, kv_count, head_dim)
        logit_scores = (
            jnp.einsum(
                "luqf,euf->uqle", query_half_rows, key_projected, preferred_element_type=jnp.float32
            )
            * inverse_scale_factor
        )
        key_pos = jnp.arange(extent, dtype=jnp.int32)
        causal = key_pos[None, :] <= query_pos[:, None]
        logit_scores = jnp.where(causal, logit_scores, neg_fill)
        new_max = jnp.maximum(running_max, jnp.max(logit_scores, axis=-1))
        attention_probabilities = jnp.where(causal, jnp.exp(logit_scores - new_max[..., None]), 0.0)
        new_sum = jnp.sum(attention_probabilities, axis=-1)
        gained = jnp.einsum(
            "vemi,iva->mvea",
            attention_probabilities.astype(jnp.bfloat16),
            value_projected,
            preferred_element_type=jnp.float32,
        )
        return (new_max, new_sum, gained)

    def keep_state():
        return (running_max, running_sum, weighted)

    return lax.cond(first_row > query_pos[-1], keep_state, update)


def finish(carried):
    running_max, running_sum, weighted = carried
    attention_mixed = weighted / jnp.transpose(running_sum, (2, 0, 1))[..., None]
    return attention_mixed.astype(jnp.bfloat16).reshape(weighted.shape[0], -1)


def local(
    x_stream,
    z_stream,
    conv_kernel,
    conv_bias,
    delta_down,
    state_proj,
    delta_up,
    delta_bias,
    log_decay,
    skip_gain,
    queries,
    key_heads,
    values,
    out_proj,
    residual,
):
    row_count = x_stream.shape[0]
    channels = x_stream.shape[1]
    rim_rows = passed_along(x_stream[row_count - (CONV - 1) :], "ctx", 1)
    padded = jnp.concatenate([rim_rows, x_stream], axis=0).astype(jnp.float32)
    convolved = conv_bias[None, :]
    for offset in range(CONV):
        convolved = convolved + conv_kernel[offset][None, :] * padded[offset : offset + row_count]
    inner_act = lax.optimization_barrier(jax.nn.silu(convolved).astype(jnp.bfloat16))
    delta_part = jnp.dot(inner_act, delta_down, preferred_element_type=jnp.float32)
    gate_part = jnp.einsum("nc,tc->nt", state_proj, inner_act, preferred_element_type=jnp.float32)
    head_count = queries.shape[1] // HD
    kv_count = key_heads.shape[1] // HD
    group_size = head_count // kv_count
    half_rows = row_count // 2
    device = lax.axis_index("ctx")
    first_half = queries[:half_rows]
    second_half = queries[half_rows:]
    second_row = device * row_count + half_rows
    first_pos = device * row_count + jnp.arange(half_rows, dtype=jnp.int32)
    second_pos = second_row + jnp.arange(half_rows, dtype=jnp.int32)
    first_query = first_half.reshape(half_rows, kv_count, group_size, HD)
    second_query = second_half.reshape(half_rows, kv_count, group_size, HD)
    start_state = (
        jnp.full((kv_count, group_size, half_rows), neg_fill, jnp.float32),
        jnp.zeros((kv_count, group_size, half_rows), jnp.float32),
        jnp.zeros((half_rows, kv_count, group_size, HD), jnp.float32),
    )
    carried = (start_state, start_state)
    first_row = jnp.int32(0)
    key_piece = lax.all_gather(key_heads, "ctx", axis=0, tiled=True)
    value_piece = lax.all_gather(values, "ctx", axis=0, tiled=True)
    first_state = half_update(carried[0], first_query, first_pos, key_piece, value_piece, first_row)
    second_state = half_update(
        carried[1], second_query, second_pos, key_piece, value_piece, first_row
    )
    first_out = finish(first_state)
    second_out = finish(second_state)
    attended = jnp.concatenate([first_out, second_out], axis=0)
    partial_full = jnp.dot(
        attended,
        lax.all_gather(out_proj, "ctx", axis=1, tiled=True),
        preferred_element_type=jnp.float32,
    )
    delta_sum, gate_sum = (
        lax.psum(delta_part.astype(jnp.bfloat16), "tp").astype(jnp.float32),
        lax.psum(gate_part.astype(jnp.bfloat16), "tp").astype(jnp.float32),
    )
    own_cols = lax.psum_scatter(
        partial_full.astype(jnp.bfloat16), "tp", scatter_dimension=1, tiled=True
    ).astype(jnp.float32)
    block_out = (residual.astype(jnp.float32) + own_cols).astype(jnp.bfloat16)
    delta_low = delta_sum.astype(jnp.bfloat16)
    step_size = jax.nn.softplus(
        jnp.dot(delta_low, delta_up, preferred_element_type=jnp.float32) + delta_bias[None, :]
    )
    decay_rate = -jnp.exp(log_decay)
    act_float = inner_act.astype(jnp.float32)
    block_count = row_count // sub_len
    lower_ones = (jnp.arange(sub_len)[:, None] >= jnp.arange(sub_len)[None, :]).astype(jnp.float32)
    in_gates = gate_sum[:NS].T.reshape(block_count, sub_len, NS)
    out_gates = gate_sum[NS:].T.reshape(block_count, sub_len, NS)
    step_blocks = step_size.reshape(block_count, sub_len, channels)
    act_blocks = act_float.reshape(block_count, sub_len, channels)
    highest = lax.Precision.HIGHEST

    def local_block(carried, inputs):
        step_row, act_row, in_gate, out_gate = inputs
        log_decays = jnp.einsum(
            "ts,snc->tnc", lower_ones, decay_rate[None] * step_row[:, None, :], precision=highest
        )
        injected = jnp.exp(-log_decays) * in_gate[:, :, None] * (step_row * act_row)[:, None, :]
        gathered_in = jnp.einsum("ts,snc->tnc", lower_ones, injected, precision=highest)
        states = jnp.exp(log_decays) * (carried[None] + gathered_in)
        return (
            states[-1],
            (jnp.einsum("tn,tnc->tc", out_gate, states, precision=highest), log_decays),
        )

    end_state, (local_out, log_blocks) = lax.scan(
        local_block,
        jnp.zeros((NS, channels), jnp.float32),
        (step_blocks, act_blocks, in_gates, out_gates),
    )
    total_decay = jnp.exp(decay_rate * jnp.sum(step_size, axis=0)[None, :])

    def chain_states(earlier, later):
        return (earlier[0] * later[0], later[0] * earlier[1] + later[1])

    neutral = (jnp.ones_like(total_decay), jnp.zeros_like(end_state))
    _, incoming = prefix((total_decay, end_state), "ctx", chain_states, neutral)

    def carry_block(carried, inputs):
        log_decays, out_gate = inputs
        states = jnp.exp(log_decays) * carried[None]
        return (states[-1], jnp.einsum("tn,tnc->tc", out_gate, states, precision=highest))

    _, carried_out = lax.scan(carry_block, incoming, (log_blocks, out_gates))
    scanned = (local_out + carried_out).reshape(row_count, channels)
    mixer_out = (
        (scanned + skip_gain[None, :] * act_float) * jax.nn.silu(z_stream.astype(jnp.float32))
    ).astype(jnp.bfloat16)
    return (mixer_out, block_out)


def solution(mesh):
    placed = (
        P("ctx", "tp"),
        P("ctx", "tp"),
        P(None, "tp"),
        P("tp"),
        P("tp", None),
        P(None, "tp"),
        P(None, "tp"),
        P("tp"),
        P(None, "tp"),
        P("tp"),
        P("ctx", "tp"),
        P("ctx", "tp"),
        P("ctx", "tp"),
        P("tp", "ctx"),
        P("ctx", "tp"),
    )
    return jax.shard_map(
        local,
        mesh=mesh,
        in_specs=placed,
        out_specs=(P("ctx", "tp"), P("ctx", "tp")),
        check_vma=False,
    )
```

profile of v0, /device:TPU:1, one launch (start us, length us, event | category | flops | bytes accessed | tf_op | source)
XLA Modules:
  0.0 559.4 jit_solution(11973186031970108383)
XLA Ops:
  9.0 4.9 collective-permute-start
  20.6 8.8 %psum.15 = bf16[32,128]{1,0:T(8,128)(2,1)S(1)} all-reduce(bf16[32,128]{1,0:T(8,128)(2,1)S(1)} %fusion.59), channel_id=1, replica_groups=mesh['ctx'=64,'tp'=4] {'tp'}, use_global_device_ids=true, to_apply=%region_1.2 | all-reduce | flops 4096 | bytes 16384 | tf_op jit(solution)/shard_map/psum | solution.py:144
  30.7 36.2 %all-reduce.2.cloned.1.call-done = bf16[128,256]{1,0:T(8,128)(2,1)} async-done(((bf16[128,256]{1,0:T(8,128)(2,1)}), bf16[128,256]{1,0:T(8,128)(2,1)}) %all-reduce.2.cloned.1.call-update) | async-done | bytes 65552 | tf_op jit(solution)/shard_map/psum | solution.py:143
  70.4 83.8 %while.43 = (s32[]{:T(128)}, f32[16,2048]{1,0:T(8,128)S(1)}, f32[8,16,2048]{2,1,0:T(8,128)S(1)}, f32[8,16,16,2048]{3,1,2,0:T(8,128)}, f32[16,2048]{1,0:T(8,128)S...) while((s32[]{:T(128)}, f32[16,2048]{1,0:T(8,128)S(1)}, ...), condition=%wide.region_3.4_spmd.clone.clone, body=%wide.region_2.3_spmd.clone.clone.sunk | while | flops 210797568 | bytes 12589689 | solution.py:177
  102.8 3.4 bitcast_dynamic-update-slice_fusion.7
  113.3 3.4 bitcast_dynamic-update-slice_fusion.7
  158.3 26.8 %all-gather.8.cloned.1.call-done = bf16[8192,256]{1,0:T(8,128)(2,1)} async-done(((bf16[128,256]{1,0:T(8,128)(2,1)}), bf16[8192,256]{1,0:T(8,128)(2,1)}) %all-gather.8.cloned.1.call-update) | async-done | bytes 4194320 | tf_op jit(solution)/shard_map/all_gather | solution.py:128
  185.1 44.1 %conditional.3 = (f32[2,4,64]{2,1,0:T(4,128)S(1)}, f32[64,2,4,128]{3,0,2,1:T(8,128)S(1)}) conditional(s32[]{:T(128)} %bitcast.29, (s32[64]{0:T(128)S(1)}, bf16[8192,256]{1,0:T(8,128)(2,1)}, bf16[128,1024]{1,0:T(8,128)(2,1)S(1)}, bf16[8192,256]{1,0:T(8,128)(2,1)}) %tuple.133, () %tuple.52), branch_computations={%region_13.16_spmd, %region_16.17_spmd} | conditional | flops 2202533376 | bytes 78524688 | solution.py:73
  185.5 6.9 %reshape.74 = bf16[8192,2,128]{2,1,0:T(2,128)(2,1)} reshape(bf16[8192,256]{1,0:T(8,128)(2,1)} %get-tuple-element.198) | data formatting | bytes 8388608 | tf_op jit(solution)/shard_map/cond/branch_0_fun/reshape | solution.py:48
  192.4 11.3 %fusion.22 = (f32[2,4,64]{2,1,0:T(4,128)S(1)}, f32[2,8192,64,4]{1,2,3,0:T(8,128)}) fusion(pred[64,8192]{1,0:T(8,128)(4,1)S(1)} %iota_compare_fusion.1, bf16[64,2,4,128]{3,2,1,0:T(4,128)(2,1)S(1)} %reshape.75, bf16[8192,2,128,1]{2,1,0,3:T(2,128)(2,1)} %bitcast.184), kind=kOutput, calls=%fused_computation.27 | convolution fusion | flops 1086324224 | bytes 21628928 | tf_op jit(solution)/shard_map/cond/branch_0_fun/luqf,euf->uqle/dot_general | solution.py:51
  203.7 6.9 %reshape.76 = bf16[8192,2,128]{2,1,0:T(2,128)(2,1)} reshape(bf16[8192,256]{1,0:T(8,128)(2,1)} %get-tuple-element.200) | data formatting | bytes 8388608 | tf_op jit(solution)/shard_map/cond/branch_0_fun/reshape | solution.py:49
  210.7 10.1 %fusion.31 = f32[64,2,4,128]{3,0,2,1:T(8,128)S(1)} fusion(bf16[8192,2,128,1]{2,1,0,3:T(2,128)(2,1)} %bitcast.186, f32[2,8192,64,4]{1,2,3,0:T(8,128)} %get-tuple-element.352, f32[2,4,64]{2,1,0:T(4,128)S(1)} %broadcast_maximum_fusion.1, pred[64,8192]{1,0:T(8,128)(4,1)S(1)} %iota_compare_fusion.1), kind=kOutput, calls=%fused_computation.36 | convolution fusion | flops 1094713344 | bytes 21760000 | tf_op jit(solution)/shard_map/cond/branch_0_fun/vemi,iva->mvea/dot_general | solution.py:62
  220.7 8.4 %fusion.24 = f32[2,4,64]{2,1,0:T(4,128)S(1)} fusion(f32[2,8192,64,4]{1,2,3,0:T(8,128)} %get-tuple-element.352, f32[2,4,64]{2,1,0:T(4,128)S(1)} %broadcast_maximum_fusion.1, pred[64,8192]{1,0:T(8,128)(4,1)S(1)} %iota_compare_fusion.1), kind=kLoop, calls=%fused_computation.29 | loop fusion | flops 20971008 | bytes 17305600 | tf_op jit(solution)/shard_map/cond/branch_0_fun/reduce_sum | solution.py:61
  229.5 44.9 %conditional.2 = (f32[2,4,64]{2,1,0:T(4,128)S(1)}, f32[64,2,4,128]{3,0,2,1:T(8,128)S(1)}) conditional(s32[]{:T(128)} %bitcast.27, (s32[64]{0:T(128)S(1)}, bf16[8192,256]{1,0:T(8,128)(2,1)}, bf16[128,1024]{1,0:T(8,128)(2,1)S(1)}, bf16[8192,256]{1,0:T(8,128)(2,1)}) %tuple.134, () %tuple.50), branch_computations={%region_9.0_spmd, %region_12.13_spmd} | conditional | flops 2202533376 | bytes 78524688 | solution.py:73
  230.1 7.1 %reshape.71 = bf16[8192,2,128]{2,1,0:T(2,128)(2,1)} reshape(bf16[8192,256]{1,0:T(8,128)(2,1)} %get-tuple-element.194) | data formatting | bytes 8388608 | tf_op jit(solution)/shard_map/cond/branch_0_fun/reshape | solution.py:48
  237.3 11.3 %fusion.4 = (f32[2,4,64]{2,1,0:T(4,128)S(1)}, f32[2,8192,64,4]{1,2,3,0:T(8,128)}) fusion(pred[64,8192]{1,0:T(8,128)(4,1)S(1)} %iota_compare_fusion, bf16[64,2,4,128]{3,2,1,0:T(4,128)(2,1)S(1)} %reshape.72, bf16[8192,2,128,1]{2,1,0,3:T(2,128)(2,1)} %bitcast.185), kind=kOutput, calls=%fused_computation.10 | convolution fusion | flops 1086324224 | bytes 21628928 | tf_op jit(solution)/shard_map/cond/branch_0_fun/luqf,euf->uqle/dot_general | solution.py:51
  248.6 7.0 %reshape.73 = bf16[8192,2,128]{2,1,0:T(2,128)(2,1)} reshape(bf16[8192,256]{1,0:T(8,128)(2,1)} %get-tuple-element.196) | data formatting | bytes 8388608 | tf_op jit(solution)/shard_map/cond/branch_0_fun/reshape | solution.py:49
  255.5 10.2 %fusion.13 = f32[64,2,4,128]{3,0,2,1:T(8,128)S(1)} fusion(bf16[8192,2,128,1]{2,1,0,3:T(2,128)(2,1)} %bitcast.187, f32[2,8192,64,4]{1,2,3,0:T(8,128)} %get-tuple-element.350, f32[2,4,64]{2,1,0:T(4,128)S(1)} %broadcast_maximum_fusion, pred[64,8192]{1,0:T(8,128)(4,1)S(1)} %iota_compare_fusion), kind=kOutput, calls=%fused_computation.19 | convolution fusion | flops 1094713344 | bytes 21760000 | tf_op jit(solution)/shard_map/cond/branch_0_fun/vemi,iva->mvea/dot_general | solution.py:62
  265.8 8.4 %fusion.6 = f32[2,4,64]{2,1,0:T(4,128)S(1)} fusion(f32[2,8192,64,4]{1,2,3,0:T(8,128)} %get-tuple-element.350, f32[2,4,64]{2,1,0:T(4,128)S(1)} %broadcast_maximum_fusion, pred[64,8192]{1,0:T(8,128)(4,1)S(1)} %iota_compare_fusion), kind=kLoop, calls=%fused_computation.12 | loop fusion | flops 20971008 | bytes 17305600 | tf_op jit(solution)/shard_map/cond/branch_0_fun/reduce_sum | solution.py:61
  274.8 7.3 %convolution_convert_fusion = bf16[128,4096]{1,0:T(8,128)(2,1)} fusion(bf16[1024,4096]{0,1:T(8,128)(2,1)} %all-gather.12.cloned.1.call-done, bf16[64,1024]{1,0:T(8,128)(2,1)S(1)} %reshape.90, bf16[64,1024]{1,0:T(8,128)(2,1)S(1)} %reshape.89), kind=kOutput, calls=%fused_computation.73 | convolution fusion | flops 1074790400 | bytes 9699328 | tf_op jit(solution)/shard_map/dot_general | solution.py:137
  282.1 70.9 %all-gather.16.cloned.1.call-done = f32[1024,2048]{1,0:T(8,128)} async-done(((f32[16,2048]{1,0:T(8,128)}), f32[1024,2048]{1,0:T(8,128)}) %all-gather.16.cloned.1.call-update) | async-done | bytes 8388624 | tf_op jit(solution)/shard_map/all_gather | solution.py:25
  353.0 84.0 %all-gather.14.cloned.1.call-done = f32[1024,2048]{1,0:T(8,128)} async-done(((f32[16,2048]{1,0:T(8,128)}), f32[1024,2048]{1,0:T(8,128)}) %all-gather.14.cloned.1.call-update) | async-done | bytes 8388624 | tf_op jit(solution)/shard_map/all_gather | solution.py:25
  437.0 69.9 %while.44 = (s32[]{:T(128)}, f32[16,2048]{1,0:T(8,128)S(1)}, s32[]{:T(128)}, f32[64,16,2048]{2,1,0:T(8,128)}, f32[64,16,2048]{2,1,0:T(8,128)}, /*index=5*/s32[]{:T(128)}, s32[]{:T(128)}) while((s32[]{:T(128)}, f32[16,2048]{1,0:T(8,128)S(1)}, s32[]{:T(128)}, f32[64,16,2048]{2,1,0:T(8,128)}, f32[64,16,2048]{2,1,0:T(8,128)}, ...), condition=%wide.region_6.7_spmd.clone, body=%wide.region_5.6_spmd.clone.sunk | while | flops 131076 | bytes 524389 | solution.py:37
  508.0 39.4 %while.42 = (s32[]{:T(128)}, f32[16,2048]{1,0:T(8,128)S(1)}, f32[8,16,2048]{2,1,0:T(8,128)}, f32[8,16,16,2048]{3,1,2,0:T(8,128)}, f32[8,16,16]{2,1,0:T(8,128)S(1)}, /*index=5*/s32[]{:T(128)}) while((s32[]{:T(128)}, f32[16,2048]{1,0:T(8,128)S(1)}, f32[8,16,2048]{2,1,0:T(8,128)}, f32[8,16,16,2048]{3,1,2,0:T(8,128)}, f32[8,16,16]{2,1,0:T(8,128)S(1)}, ...), condition=%wide.region_8.9_spmd, body=%wide.region_7.8_spmd.sunk | while | flops 6815746 | bytes 11275853 | solution.py:195
  (269 shorter events, 205.8 us)
Async XLA Ops:
  8.0 59.0 %copy-start = (bf16[256,2048]{1,0:T(8,128)(2,1)S(1)}, bf16[256,2048]{1,0:T(8,128)(2,1)}, u32[]{:S(2)}) copy-start(bf16[256,2048]{1,0:T(8,128)(2,1)} %param.31) | copy-start | bytes 3145732
  8.0 9.5 %copy-start.3 = (bf16[2048,256]{1,0:T(8,128)(2,1)S(1)}, bf16[2048,256]{1,0:T(8,128)(2,1)}, u32[]{:S(2)}) copy-start(bf16[2048,256]{1,0:T(8,128)(2,1)} %param.29) | copy-start | bytes 3145732
  8.0 58.9 %all-reduce.2.cloned.1.call-start = ((), (), s32[]{:S(2)}) async-start(), calls=%async_computation.1 | async-start | bytes 131072 | tf_op jit(solution)/shard_map/psum | solution.py:143
  9.0 5.9 %collective-permute-start = (bf16[3,2048]{1,0:T(4,128)(2,1)S(1)}, bf16[3,2048]{1,0:T(4,128)(2,1)S(1)}, u32[]{:S(2)}, u32[]{:S(2)}) collective-permute-start(bf16[3,2048]{1,0:T(4,128)(2,1)S(1)} %slice.54), channel_id=1, source_target_pairs={{0,4},{4,8},{8,12},{12,16},{16,20},{20,24},{24,28},{28,32},{32,36}... | collective-permute-start | bytes 36872 | tf_op jit(solution)/shard_map/ppermute | solution.py:20
  14.9 5.4 copy-start.8
  16.1 50.8 %copy-start.10 = (f32[2048]{0:T(1024)S(1)}, f32[2048]{0:T(1024)}, u32[]{:S(2)}) copy-start(f32[2048]{0:T(1024)} %param.32) | copy-start | bytes 24580
  17.5 52.1 %copy-start.7 = (f32[16,2048]{1,0:T(8,128)S(1)}, f32[16,2048]{1,0:T(8,128)}, u32[]{:S(2)}) copy-start(f32[16,2048]{1,0:T(8,128)} %param.33) | copy-start | bytes 393220
  18.5 139.8 %all-gather.10.cloned.1.call-start = ((), (), s32[]{:S(2)}) async-start(), calls=%async_computation.3 | async-start | bytes 4259840 | tf_op jit(solution)/shard_map/all_gather | solution.py:129
  19.1 166.0 %all-gather.8.cloned.1.call-start = ((), (), s32[]{:S(2)}) async-start(), calls=%async_computation.2 | async-start | bytes 4259840 | tf_op jit(solution)/shard_map/all_gather | solution.py:128
  19.7 255.1 %all-gather.12.cloned.1.call-start = ((), (), s32[]{:S(2)}) async-start(), calls=%async_computation.4 | async-start | bytes 8519680 | tf_op jit(solution)/shard_map/all_gather | solution.py:139
  20.3 332.8 %all-gather.16.cloned.1.call-start = ((), (), s32[]{:S(2)}) async-start(), calls=%async_computation.7 | async-start | bytes 8519680 | tf_op jit(solution)/shard_map/all_gather | solution.py:25
  70.4 114.7 %copy-start.6 = (bf16[128,1024]{1,0:T(8,128)(2,1)S(1)}, bf16[128,1024]{1,0:T(8,128)(2,1)}, u32[]{:S(2)}) copy-start(bf16[128,1024]{1,0:T(8,128)(2,1)} %param.35) | copy-start | bytes 786436
  154.2 0.7 copy-start.2
  154.9 282.1 %all-gather.14.cloned.1.call-start = ((), (), s32[]{:S(2)}) async-start(), calls=%async_computation.6 | async-start | bytes 8519680 | tf_op jit(solution)/shard_map/all_gather | solution.py:25
  155.7 394.5 %reduce-scatter.2.cloned.1.call-start = ((), (), s32[]{:S(2)}) async-start(), calls=%async_computation.5 | async-start | bytes 1310720 | tf_op jit(solution)/shard_map/reduce_scatter | solution.py:146
  508.0 40.9 %copy-start.4 = (bf16[128,2048]{1,0:T(8,128)(2,1)S(1)}, bf16[128,2048]{1,0:T(8,128)(2,1)}, u32[]{:S(2)}) copy-start(bf16[128,2048]{1,0:T(8,128)(2,1)} %param.26) | copy-start | bytes 1572868
  508.0 40.9 %copy-start.9 = (f32[2048]{0:T(1024)S(1)}, f32[2048]{0:T(1024)}, u32[]{:S(2)}) copy-start(f32[2048]{0:T(1024)} %param.34) | copy-start | bytes 24580
  547.4 2.7 copy-start.5
  547.5 4.4 copy-start.1
Sparse Core Ops, SparseCore 0:
  18.6 48.2 all-reduce.1
  282.2 21.9 reduce-scatter.1
Sparse Core Ops, SparseCore 1:
  22.1 84.0 all-gather.9
  109.3 75.8 all-gather.7
  188.1 80.9 all-gather.11
  272.8 80.1 all-gather.15
  356.8 80.2 all-gather.13
where the time goes:
time: 562 us; the launch traced here: 559 us
  waiting for transfers between devices  220 us (39%)
  matrix products  129 us (23%)
  other arithmetic  113 us (20%)
  local copies, waits for them, and re-layouts  62.4 us (11%)
  between operations  17.3 us (3%)
  blocking collectives  8.85 us (2%)
    all_gather x2, waiting for transfers between devices, prefix(): everything = jax.tree.map(lambda part: lax.all_gather(part, axis), value)  155 us
    select_n x64, other arithmetic, lap(): return jax.tree.map(lambda a, b: jnp.where(reached, a, b), new, before)  68.5 us
    psum x1, waiting for transfers between devices, local(): lax.psum(delta_part.astype(jnp.bfloat16), 'tp').astype(jnp.float32)  36.2 us
    dot_general x8, matrix products, local_block(): jnp.einsum('ts,snc->tnc', lower_ones, decay_rate[None] * step_row[:, None...  27 us
    all_gather x1, waiting for transfers between devices, local(): key_piece = lax.all_gather(key_heads, 'ctx', axis=0, tiled=True)  26.8 us
    dot_general x2, matrix products, update(): jnp.einsum('luqf,euf->uqle', query_half_rows, key_projected, preferred_el...  22.6 us
    dot_general x8, matrix products, local_block(): jnp.einsum('ts,snc->tnc', lower_ones, injected, precision=highest)  21.2 us
    dot_general x2, matrix products, update(): jnp.einsum('vemi,iva->mvea', attention_probabilities.astype(jnp.bfloat16)...  20.3 us
  transfers between devices with their start and end apart: 8, of which 4 were waited for; matrix products, arithmetic and copies ran while one was open for 53% of the time, Pallas kernels for 0%

commit v1 on v0

v1 whole, which is shorter than its diff:
```python
import math

import jax
import jax.numpy as jnp
from jax import lax
from jax.experimental import pallas as pl
from jax.experimental.pallas import tpu as pltpu
from jax.sharding import PartitionSpec as P

HD = 128
BF = jnp.bfloat16
F32 = jnp.float32
MESH = pl.DeviceIdType.MESH
NS = 16
LOG2E = math.log2(math.e)
SCALE = math.log2(math.e) / math.sqrt(HD)


def at(ctx, tp):
    return {"ctx": ctx, "tp": tp}


def ctx_of(x, z, core):
    return (x * 8 + z) * 2 + core


def ring_position(x, z, core):
    first = 4 * z + (x + z) % 4
    turn = (z + 5 * x) % 8
    second = 4 * (x + 4 * (turn // 4)) + turn % 4
    return (1 - core) * first + core * second


def ring_chip(position, core):
    major = position // 4
    minor = position % 4
    x = (1 - core) * ((minor + 3 * major) % 4) + core * (major % 4)
    z = (1 - core) * major + core * ((3 * major + minor) % 8)
    return x, z


def attn_kernel(
    q_ref, k_ref, v_ref, wt_ref, res_ref, out_ref,
    qts, vts, qt, kbuf, vtbuf, wbuf, m_ref, l_ref, acc, att, stage, landed, out_t,
    pair_send, pair_recv, ring_send, ring_recv, y_send, y_recv,
):
    me = lax.axis_index("ctx")
    y = lax.axis_index("tp")
    core = me % 2
    other = 1 - core
    z = (me // 2) % 8
    x = me // 16
    chip = me // 2
    partner = at(me + 1 - 2 * core, y)
    here = ring_position(x, z, core)
    xr, zr = ring_chip((here + 1) % 32, core)
    xl, zl = ring_chip((here + 31) % 32, core)
    right = at(ctx_of(xr, zr, core), y)
    left = at(ctx_of(xl, zl, core), y)

    barrier = pltpu.get_barrier_semaphore()
    for peer in (partner, right, left):
        pl.semaphore_signal(barrier, inc=1, device_id=peer, device_id_type=MESH)
    for step in (1, 2, 3):
        for r in range(2):
            pl.semaphore_signal(
                barrier, inc=1, device_id=at(chip * 2 + r, (y + step) % 4), device_id_type=MESH
            )
    for g in range(2):
        for h in range(4):
            head = q_ref[:, (g * 4 + h) * HD:(g * 4 + h + 1) * HD]
            qts[g, :, h * HD:(h + 1) * HD] = head.astype(F32).T.astype(BF)
    vts[...] = v_ref[...].astype(F32).T.astype(BF)
    pl.semaphore_wait(barrier, 9)

    own_rows = pl.ds(pl.multiple_of(core * 128, 128), 128)
    other_rows = pl.ds(pl.multiple_of(other * 128, 128), 128)
    own_cols = pl.ds(pl.multiple_of(core * 512, 512), 512)

    def pair_copy(src, dst, k):
        return pltpu.make_async_remote_copy(
            src_ref=src, dst_ref=dst, send_sem=pair_send.at[k], recv_sem=pair_recv.at[k],
            device_id=partner, device_id_type=MESH,
        )

    swaps = (
        pair_copy(k_ref.at[:, other_rows], kbuf.at[0, own_rows, :], 0),
        pair_copy(vts.at[other_rows, :], vtbuf.at[0, :, own_rows], 1),
        pair_copy(qts.at[other], qt.at[:, own_cols], 2),
    )
    for swap in swaps:
        swap.start()
    kbuf[0, own_rows, :] = k_ref[:, own_rows]
    vtbuf[0, :, own_rows] = vts[own_rows, :]
    qt[:, own_cols] = qts[core]
    wbuf[0] = wt_ref[...]
    m_ref[...] = jnp.full_like(m_ref, -1e30)
    l_ref[...] = jnp.zeros_like(l_ref)
    acc[...] = jnp.zeros_like(acc)
    bufs = (kbuf, vtbuf, wbuf)

    def ring_copy(kind, src, dst, peer):
        buf = bufs[kind]
        return pltpu.make_async_remote_copy(
            src_ref=buf.at[src], dst_ref=buf.at[dst],
            send_sem=ring_send.at[kind, dst], recv_sem=ring_recv.at[kind, dst],
            device_id=peer, device_id_type=MESH,
        )

    for kind in (0, 1):
        swaps[kind].wait()
        ring_copy(kind, 0, 1, right).start()
        ring_copy(kind, 0, 2, left).start()
    ring_copy(2, 0, 1, right).start()
    ring_copy(2, 0, 2, left).start()
    swaps[2].wait()

    def attend(slot, masked):
        for j in range(4):
            cols = pl.ds(j * 256, 256)
            s = jnp.dot(kbuf[slot], qt[:, cols], preferred_element_type=F32) * SCALE
            if masked:
                key = lax.broadcasted_iota(jnp.int32, (256, 256), 0)
                row = lax.broadcasted_iota(jnp.int32, (256, 256), 1) % 128 + (j // 2) * 128
                s = jnp.where(key <= row, s, -1e30)
            m_old = m_ref[:, cols]
            m_new = jnp.maximum(m_old, jnp.max(s, axis=0, keepdims=True))
            p = jnp.exp2(s - m_new)
            alpha = jnp.exp2(m_old - m_new)
            m_ref[:, cols] = m_new
            l_ref[:, cols] = l_ref[:, cols] * alpha + jnp.sum(p, axis=0, keepdims=True)
            acc[:, cols] = acc[:, cols] * alpha + jnp.dot(
                vtbuf[slot], p.astype(BF), preferred_element_type=F32
            )

    attend(0, True)

    def origin(slot_step, sign):
        return ring_chip((here + 32 - sign * slot_step) % 32, core)

    def step(s, _):
        plus, minus = 2 * s - 1, 2 * s
        for kind in (0, 1):
            ring_copy(kind, 0, plus, right).wait_recv()

            @pl.when(s < 16)
            def _():
                ring_copy(kind, plus, plus + 2, right).start()

                ring_copy(kind, 0, minus, left).wait_recv()

            @pl.when(s < 15)
            def _():
                ring_copy(kind, minus, minus + 2, left).start()

        xo, zo = origin(s, 1)

        @pl.when(xo * 8 + zo < chip)
        def _():
            attend(plus, False)

        xo, zo = origin(s, -1)

        @pl.when((s < 16) & (xo * 8 + zo < chip))
        def _():
            attend(minus, False)

        ring_copy(2, 0, plus, right).wait_recv()

        @pl.when(s < 16)
        def _():
            ring_copy(2, plus, plus + 2, right).start()
            ring_copy(2, 0, minus, left).wait_recv()

        @pl.when(s < 15)
        def _():
            ring_copy(2, minus, minus + 2, left).start()

        return 0

    lax.fori_loop(1, 17, step, 0)

    inverse = 1.0 / l_ref[...]
    own_feats = pl.ds(pl.multiple_of(core * 512, 512), 512)
    att_own = []
    for h in range(4):
        pieces = []
        for r in range(2):
            cols = slice(r * 512 + h * 128, r * 512 + (h + 1) * 128)
            pieces.append((acc[:, cols] * inverse[:, cols]).astype(BF))
        att_own.append(jnp.concatenate(pieces, axis=1))
    att[own_feats, :] = jnp.concatenate(att_own, axis=0)
    swap = pair_copy(att.at[own_feats, :], att.at[own_feats, :], 3)
    swap.start()
    swap.wait()

    def project(slot, xo, zo):
        part = jnp.dot(wbuf[slot], att[...], preferred_element_type=F32).astype(BF)
        rows = pl.ds(pl.multiple_of(zo * 64, 64), 64)
        stage[xo, 0, rows, :] = part[:, :128]
        stage[xo, 1, rows, :] = part[:, 128:]

    project(0, x, z)

    def project_step(s, _):
        xo, zo = origin(s, 1)
        project(2 * s - 1, xo, zo)
        xo, zo = origin(s, -1)

        @pl.when(s < 16)
        def _():
            project(2 * s, xo, zo)

        return 0

    lax.fori_loop(1, 17, project_step, 0)

    def y_copy(gap, r):
        there = (y + gap) % 4
        k = gap * 2 + r
        return pltpu.make_async_remote_copy(
            src_ref=stage.at[there, r], dst_ref=landed.at[gap, core],
            send_sem=y_send.at[k], recv_sem=y_recv.at[gap, core],
            device_id=at(chip * 2 + r, there), device_id_type=MESH,
        )

    def y_arrival(gap, c):
        return pltpu.make_async_remote_copy(
            src_ref=stage.at[0, 0], dst_ref=landed.at[gap, c],
            send_sem=y_send.at[0], recv_sem=y_recv.at[gap, c],
            device_id=partner, device_id_type=MESH,
        )

    for gap in (2, 1, 3):
        for r in range(2):
            y_copy(gap, r).start()
    swap = pltpu.make_async_remote_copy(
        src_ref=stage.at[y, other], dst_ref=landed.at[0, core],
        send_sem=y_send.at[0], recv_sem=y_recv.at[0, core],
        device_id=partner, device_id_type=MESH,
    )
    swap.start()
    landed[0, core] = stage[y, core]
    y_arrival(0, other).wait_recv()
    for gap in (1, 3, 2):
        for c in range(2):
            y_arrival(gap, c).wait_recv()
    total = landed[0].astype(F32)
    for gap in range(1, 4):
        total = total + landed[gap].astype(F32)
    for zo in range(8):
        for c in range(2):
            out_t[zo * 128 + c * 64:zo * 128 + c * 64 + 64, :] = total[c, zo * 64:zo * 64 + 64, :]
    for zo in range(8):
        cols = slice(zo * 128, (zo + 1) * 128)
        out_ref[:, cols] = (res_ref[:, cols].astype(F32) + out_t[cols, :].T).astype(BF)
    swap.wait_send()
    for gap in (1, 2, 3):
        for r in range(2):
            y_copy(gap, r).wait_send()

    def drain(s, _):
        for kind in range(3):
            ring_copy(kind, 0, 2 * s - 1, right).wait_send()

            @pl.when(s < 16)
            def _():
                ring_copy(kind, 0, 2 * s, left).wait_send()

        return 0

    lax.fori_loop(1, 17, drain, 0)


def attention(queries, key_heads, values, out_proj, residual):
    vmem = pl.BlockSpec(memory_space=pltpu.VMEM)
    return pl.pallas_call(
        attn_kernel,
        out_shape=jax.ShapeDtypeStruct(residual.shape, BF),
        in_specs=[vmem] * 5,
        out_specs=vmem,
        scratch_shapes=[
            pltpu.VMEM((2, 128, 512), BF),
            pltpu.VMEM((256, 128), BF),
            pltpu.VMEM((128, 1024), BF),
            pltpu.VMEM((32, 256, 128), BF),
            pltpu.VMEM((32, 128, 256), BF),
            pltpu.VMEM((32, 64, 1024), BF),
            pltpu.VMEM((1, 1024), F32),
            pltpu.VMEM((1, 1024), F32),
            pltpu.VMEM((128, 1024), F32),
            pltpu.VMEM((1024, 256), BF),
            pltpu.VMEM((4, 2, 512, 128), BF),
            pltpu.VMEM((4, 2, 512, 128), BF),
            pltpu.VMEM((1024, 128), F32),
            pltpu.SemaphoreType.DMA((4,)),
            pltpu.SemaphoreType.DMA((4,)),
            pltpu.SemaphoreType.DMA((3, 32)),
            pltpu.SemaphoreType.DMA((3, 32)),
            pltpu.SemaphoreType.DMA((8,)),
            pltpu.SemaphoreType.DMA((4, 2)),
        ],
        compiler_params=pltpu.CompilerParams(
            collective_id=0, has_side_effects=True, vmem_limit_bytes=48 * 1024 * 1024
        ),
    )(queries, key_heads, values, out_proj.T, residual)


def ssm_kernel(
    x_ref, z_ref, ck_ref, cb_ref, dd_ref, sp_ref, du_ref, db_ref, ld_ref, sg_ref, out_ref,
    rim, padded, act, dpart, gpart, dland, gland, gsum, gates, steps, inject, scanned, decay,
    ends, total, ends_in, total_in, before, shift, column, column_in, entry_out, entry,
    rim_send, rim_recv, tp_send, tp_recv, col_send, col_recv, x_send, x_recv, back_send, back_recv, local_sem,
):
    me = lax.axis_index("ctx")
    y = lax.axis_index("tp")
    x = me // 16
    k = me % 16
    after = at((me + 1) % 64, y)
    earlier = at((me + 63) % 64, y)

    def tp_peer(gap):
        return at(me, (y + gap) % 4)

    def col_peer(gap):
        return at(x * 16 + (k + gap) % 16, y)

    def x_peer(gap):
        return at(((x + gap) % 4) * 16 + k, y)

    barrier = pltpu.get_barrier_semaphore()

    def greet(peer):
        pl.semaphore_signal(barrier, inc=1, device_id=peer, device_id_type=MESH)

    greet(after)
    greet(earlier)
    for gap in (1, 2, 3):
        greet(tp_peer(gap))
        greet(x_peer(gap))
    for gap in range(1, 16):
        greet(col_peer(gap))
    padded[8:, :] = x_ref[...].astype(F32)
    pl.semaphore_wait(barrier, 23)

    def remote(src, dst, send, recv, peer):
        return pltpu.make_async_remote_copy(
            src_ref=src, dst_ref=dst, send_sem=send, recv_sem=recv, device_id=peer, device_id_type=MESH
        )

    rim_copy = remote(x_ref.at[pl.ds(112, 16), :], rim, rim_send.at[0], rim_recv.at[0], after)
    rim_copy.start()
    rate = -LOG2E * jnp.exp(ld_ref[...])
    for j in range(16):
        decay[pl.ds(j, 16, stride=16), :] = rate[:, j * 128:(j + 1) * 128]
    rim_copy.wait()
    padded[:8, :] = jnp.where(me > 0, rim[8:, :].astype(F32), 0.0)

    for c in range(8):
        cols = slice(c * 256, (c + 1) * 256)
        conv = cb_ref[:, cols]
        for tap in range(4):
            conv = conv + ck_ref[tap:tap + 1, cols] * padded[5 + tap:133 + tap, cols]
        act[:, cols] = (conv / (1.0 + jnp.exp(-conv))).astype(BF)
    dpart[...] = jnp.dot(act[...], dd_ref[...], preferred_element_type=F32).astype(BF)
    gpart[...] = lax.dot_general(
        sp_ref[...], act[...], (((1,), (1,)), ((), ())), preferred_element_type=F32
    )

    def tp_copies(gap):
        return (
            remote(dpart, dland.at[gap - 1], tp_send.at[0, gap], tp_recv.at[0, gap], tp_peer(gap)),
            remote(gpart, gland.at[gap - 1], tp_send.at[1, gap], tp_recv.at[1, gap], tp_peer(gap)),
        )

    for gap in (2, 1, 3):
        for copy in tp_copies(gap):
            copy.start()
    for gap in (1, 3, 2):
        for copy in tp_copies(gap):
            copy.wait()
    gsum[...] = gpart[...] + gland[0] + gland[1] + gland[2]
    to_scalars = pltpu.make_async_copy(gsum, gates, local_sem.at[0])
    to_scalars.start()
    low = (
        dpart[...].astype(F32) + dland[0].astype(F32) + dland[1].astype(F32) + dland[2].astype(F32)
    ).astype(BF)
    for c in range(8):
        cols = slice(c * 256, (c + 1) * 256)
        raw = jnp.dot(low, du_ref[:, cols], preferred_element_type=F32) + db_ref[:, cols]
        size = jnp.maximum(raw, 0.0) + jnp.log1p(jnp.exp(-jnp.abs(raw)))
        drive = size * act[:, cols].astype(F32)
        for half in range(2):
            j = c * 2 + half
            steps[pl.ds(j, 128, stride=16), :] = size[:, half * 128:(half + 1) * 128]
            inject[pl.ds(j, 128, stride=16), :] = drive[:, half * 128:(half + 1) * 128]
    to_scalars.wait()

    def rows_of(t):
        return pl.ds(pl.multiple_of(t * 16, 16), 16)

    for half in range(2):
        base = half * 8
        rates = [decay[(base + n) * 16:(base + n + 1) * 16, :] for n in range(8)]

        def advance(t, carried):
            size = steps[rows_of(t), :]
            drive = inject[rows_of(t), :]
            out = [
                jnp.exp2(rates[n] * size) * carried[n] + gates[base + n, t] * drive
                for n in range(8)
            ]
            return tuple(out) + (carried[8] + size,)

        zero = jnp.zeros((16, 128), F32)
        last = lax.fori_loop(0, 128, advance, (zero,) * 9, unroll=2)
        for n in range(8):
            ends[base + n] = last[n]
        if half == 0:
            total[...] = last[8]

    def col_copies(gap):
        return (
            remote(ends.at[(k + gap) % 16], ends_in.at[gap], col_send.at[0, gap], col_recv.at[0, gap], col_peer(gap)),
            remote(total, total_in.at[gap], col_send.at[1, gap], col_recv.at[1, gap], col_peer(gap)),
        )

    def col_start(gap, _):
        for copy in col_copies(gap):
            copy.start()
        return 0

    def col_wait(gap, _):
        for copy in col_copies(gap):
            copy.wait()
        return 0

    lax.fori_loop(1, 16, col_start, 0)
    ends_in[0] = ends[k]
    total_in[0] = total[...]
    my_rate = decay[rows_of(k), :]
    lax.fori_loop(1, 16, col_wait, 0)

    def chain(j, carried):
        state, sizes = carried
        before[j] = state
        shift[j] = sizes
        slot = (k + 16 - j) % 16
        size = total_in[slot]
        return (jnp.exp2(my_rate * size) * state + ends_in[slot], sizes + size)

    zero = jnp.zeros((16, 128), F32)
    state, sizes = lax.fori_loop(0, 16, chain, (zero, zero))
    column[0] = state
    column[1] = sizes

    def x_copy(gap):
        return remote(column, column_in.at[gap - 1], x_send.at[gap], x_recv.at[gap], x_peer(gap))

    for gap in (2, 1, 3):
        x_copy(gap).start()
    for gap in (1, 3, 2):
        x_copy(gap).wait()
    incoming = zero
    for xs in range(3):
        slot = jnp.minimum((x + 3 - xs) % 4, 2)
        ahead = jnp.exp2(my_rate * column_in[slot, 1]) * incoming + column_in[slot, 0]
        incoming = jnp.where(xs < x, ahead, incoming)

    def finish(j, _):
        entry_out[j] = before[j] + jnp.exp2(my_rate * shift[j]) * incoming
        return 0

    lax.fori_loop(0, 16, finish, 0)

    def back_copy(gap):
        return remote(
            entry_out.at[(k + gap) % 16], entry.at[k], back_send.at[gap], back_recv.at[gap], col_peer(gap)
        )

    def back_arrival(gap):
        return remote(
            entry_out.at[(k + gap) % 16], entry.at[(k + 16 - gap) % 16], back_send.at[gap], back_recv.at[gap], col_peer(gap)
        )

    def back_start(gap, _):
        back_copy(gap).start()
        return 0

    def back_wait(gap, _):
        back_copy(gap).wait_send()
        back_arrival(gap).wait_recv()
        return 0

    lax.fori_loop(1, 16, back_start, 0)
    entry[k] = entry_out[k]
    lax.fori_loop(1, 16, back_wait, 0)

    for half in range(2):
        base = half * 8
        rates = [decay[(base + n) * 16:(base + n + 1) * 16, :] for n in range(8)]

        def advance(t, carried):
            size = steps[rows_of(t), :]
            drive = inject[rows_of(t), :]
            out = []
            mixed = scanned[rows_of(t), :] if half else None
            for n in range(8):
                state = jnp.exp2(rates[n] * size) * carried[n] + gates[base + n, t] * drive
                term = gates[NS + base + n, t] * state
                mixed = term if mixed is None else mixed + term
                out.append(state)
            scanned[rows_of(t), :] = mixed
            return tuple(out)

        lax.fori_loop(0, 128, advance, tuple(entry[base + n] for n in range(8)), unroll=2)

    for j in range(16):
        cols = slice(j * 128, (j + 1) * 128)
        gate = z_ref[:, cols].astype(F32)
        mixed = scanned[pl.ds(j, 128, stride=16), :] + sg_ref[:, cols] * act[:, cols].astype(F32)
        out_ref[:, cols] = (mixed * (gate / (1.0 + jnp.exp(-gate)))).astype(BF)


def recurrence(
    x_stream, z_stream, conv_kernel, conv_bias, delta_down, state_proj, delta_up, delta_bias, log_decay, skip_gain
):
    vmem = pl.BlockSpec(memory_space=pltpu.VMEM)
    dma = pltpu.SemaphoreType.DMA
    return pl.pallas_call(
        ssm_kernel,
        out_shape=jax.ShapeDtypeStruct(x_stream.shape, BF),
        in_specs=[vmem] * 10,
        out_specs=vmem,
        scratch_shapes=[
            pltpu.VMEM((16, 2048), BF),
            pltpu.VMEM((136, 2048), F32),
            pltpu.VMEM((128, 2048), BF),
            pltpu.VMEM((128, 256), BF),
            pltpu.VMEM((32, 128), F32),
            pltpu.VMEM((3, 128, 256), BF),
            pltpu.VMEM((3, 32, 128), F32),
            pltpu.VMEM((32, 128), F32),
            pltpu.SMEM((32, 128), F32),
            pltpu.VMEM((2048, 128), F32),
            pltpu.VMEM((2048, 128), F32),
            pltpu.VMEM((2048, 128), F32),
            pltpu.VMEM((256, 128), F32),
            pltpu.VMEM((16, 16, 128), F32),
            pltpu.VMEM((16, 128), F32),
            pltpu.VMEM((16, 16, 128), F32),
            pltpu.VMEM((16, 16, 128), F32),
            pltpu.VMEM((16, 16, 128), F32),
            pltpu.VMEM((16, 16, 128), F32),
            pltpu.VMEM((2, 16, 128), F32),
            pltpu.VMEM((3, 2, 16, 128), F32),
            pltpu.VMEM((16, 16, 128), F32),
            pltpu.VMEM((16, 16, 128), F32),
            dma((1,)), dma((1,)), dma((2, 4)), dma((2, 4)), dma((2, 16)), dma((2, 16)),
            dma((4,)), dma((4,)), dma((16,)), dma((16,)), dma((1,)),
        ],
        compiler_params=pltpu.CompilerParams(
            collective_id=1, has_side_effects=True, vmem_limit_bytes=48 * 1024 * 1024
        ),
    )(
        x_stream, z_stream, conv_kernel, conv_bias[None, :], delta_down, state_proj, delta_up,
        delta_bias[None, :], log_decay, skip_gain[None, :],
    )


def local(
    x_stream, z_stream, conv_kernel, conv_bias, delta_down, state_proj, delta_up, delta_bias,
    log_decay, skip_gain, queries, key_heads, values, out_proj, residual,
):
    mixer_out = recurrence(
        x_stream, z_stream, conv_kernel, conv_bias, delta_down, state_proj, delta_up, delta_bias,
        log_decay, skip_gain,
    )
    block_out = attention(queries, key_heads, values, out_proj, residual)
    return mixer_out, block_out


def solution(mesh):
    both = P("ctx", "tp")
    placed = (
        both, both, P(None, "tp"), P("tp"), P("tp", None), P(None, "tp"), P(None, "tp"), P("tp"),
        P(None, "tp"), P("tp"), both, both, both, P("tp", "ctx"), both,
    )
    return jax.shard_map(
        local, mesh=mesh, in_specs=placed, out_specs=(both, both), check_vma=False
    )
```

time: 562 us -> 162 us (0.29)
  waiting for transfers between devices: 220 us -> 0 us
  Pallas kernels: 0 us -> 150 us
  matrix products: 129 us -> 0 us
  other arithmetic: 113 us -> 0 us
  local copies, waits for them, and re-layouts: 62.4 us -> 10.7 us
  between operations: 17.3 us -> 0.72 us
  blocking collectives: 8.85 us -> 0 us
    all_gather x5 -> x0, waiting for transfers between devices: 182 us -> none  [the longest x2 155 us: prefix(): everything = jax.tree.map(lambda part: lax.all_gather(part, axis), value)]
    pallas_call x0 -> x2, Pallas kernels: none -> 150 us  [the longest x1 98.8 us: attention(): pl.pallas_call(attn_kernel, out_shape=jax.ShapeDtypeStruct(residual.shape...]
    dot_general x40 -> x0, matrix products: 129 us -> none  [the longest x8 27 us: local_block(): jnp.einsum('ts,snc->tnc', lower_ones, decay_rate[None] * step_row[:, None...]
    select_n x64 -> x0, other arithmetic: 68.5 us -> none  [lap(): return jax.tree.map(lambda a, b: jnp.where(reached, a, b), new, before)]
    psum x1 -> x0, waiting for transfers between devices: 36.2 us -> none  [local(): lax.psum(delta_part.astype(jnp.bfloat16), 'tp').astype(jnp.float32)]
    reshape x9 -> x0, local copies, waits for them, and re-layouts: 28.2 us -> none  [the longest x2 14 us: update(): key_projected = key_piece.reshape(extent, kv_count, head_dim)]
    mul x16 -> x0, other arithmetic: 18.3 us -> none  [the longest x8 10.5 us: carry_block(): states = jnp.exp(log_decays) * carried[None]]
    reduce_sum x2 -> x0, other arithmetic: 16.9 us -> none  [update(): new_sum = jnp.sum(attention_probabilities, axis=-1)]
  transfers between devices with their start and end apart: 8 -> 0, of which waited for: 4 -> 0; matrix products, arithmetic and copies ran while one was open for 53% -> 0% of each run, Pallas kernels for 0% -> 0%
where the time goes in v1:
time: 162 us
  Pallas kernels  150 us (93%)
  local copies, waits for them, and re-layouts  10.7 us (7%)
    pallas_call x1, Pallas kernels, attention(): pl.pallas_call(attn_kernel, out_shape=jax.ShapeDtypeStruct(residual.shape...  98.8 us
    pallas_call x1, Pallas kernels, recurrence(): pl.pallas_call(ssm_kernel, out_shape=jax.ShapeDtypeStruct(x_stream.shape,...  51.5 us
    unnamed x32, local copies, waits for them, and re-layouts  10.7 us

profile of v1, /device:TPU:1, one launch (start us, length us, event | category | flops | bytes accessed | tf_op | source)
XLA Modules:
  0.0 161.8 jit_solution(15333992983542262132)
XLA Ops:
  0.6 0.0 copy-start
  0.6 1.2 copy-done
  1.9 0.0 copy-start.1
  1.9 1.2 copy-done.1
  3.1 0.0 copy-start.2
  3.1 1.0 copy-done.2
  4.1 0.0 copy-start.3
  4.1 1.0 copy-done.3
  5.2 0.9 copy-done.6
  6.1 0.9 copy-done.7
  7.0 0.8 copy-done.11
  7.7 0.7 copy-done.12
  8.4 0.7 copy-done.13
  9.1 0.7 copy-done.14
  9.8 0.0 copy-start.10
  9.9 51.5 %shard_map.158 = bf16[128,2048]{1,0:T(8,128)(2,1)S(1)} custom-call(bf16[128,2048]{1,0:T(8,128)(2,1)S(1)} %copy-done.2, bf16[128,2048]{1,0:T(8,128)(2,1)S(1)} %copy-done.3, f32[4,2048]{1,0:T(4,128)S(1)} %copy-done.11, f32[1,2048]{1,0:T(1,128)S(1)} %bitcast.5, bf16[2048,256]{1,0:T(8,128)(2,1)S(1)} %copy-done, bf16[32,2048]{1,0:T(8,128)(2,1)S(1)} %copy-done.6, ...), custom_call_target="tpu_custom_call" | custom-call | tf_op jit(solution)/shard_map/pallas_call | solution.py:530
  61.4 0.0 copy-done.4
  61.4 0.0 copy-done.5
  61.4 0.0 copy-done.8
  61.4 0.0 copy-done.9
  61.4 0.0 copy-done.10
  61.4 98.8 %shard_map.159 = bf16[128,1024]{1,0:T(8,128)(2,1)S(1)} custom-call(bf16[128,1024]{1,0:T(8,128)(2,1)S(1)} %copy-done.4, bf16[128,256]{1,0:T(8,128)(2,1)S(1)} %copy-done.9, bf16[128,256]{1,0:T(8,128)(2,1)S(1)} %copy-done.10, bf16[64,1024]{1,0:T(8,128)(2,1)S(1)} %bitcast.4, bf16[128,1024]{1,0:T(8,128)(2,1)S(1)} %copy-done.5), custom_call_target="tpu_custom_call" | custom-call | tf_op jit(solution)/shard_map/pallas_call | solution.py:277
  160.3 0.8 copy.19
  161.1 0.7 copy.20
  (10 shorter events, 0.0 us)
Async XLA Ops:
  0.6 1.2 copy-start
  1.9 1.2 copy-start.1
  3.1 1.0 copy-start.2
  4.1 1.0 copy-start.3
  5.2 0.9 copy-start.6
  6.1 0.9 copy-start.7
  7.0 0.8 copy-start.11
  7.7 0.7 copy-start.12
  8.4 0.7 copy-start.13
  9.1 0.7 copy-start.14
  9.8 51.5 %copy-start.4 = (bf16[128,1024]{1,0:T(8,128)(2,1)S(1)}, bf16[128,1024]{1,0:T(8,128)(2,1)}, u32[]{:S(2)}) copy-start(bf16[128,1024]{1,0:T(8,128)(2,1)} %q_ref.1) | copy-start | bytes 786436
  9.8 51.5 %copy-start.5 = (bf16[128,1024]{1,0:T(8,128)(2,1)S(1)}, bf16[128,1024]{1,0:T(8,128)(2,1)}, u32[]{:S(2)}) copy-start(bf16[128,1024]{1,0:T(8,128)(2,1)} %res_ref.1) | copy-start | bytes 786436
  9.8 51.5 %copy-start.8 = (bf16[1024,64]{0,1:T(8,128)(2,1)S(1)}, bf16[1024,64]{0,1:T(8,128)(2,1)}, u32[]{:S(2)}) copy-start(bf16[1024,64]{0,1:T(8,128)(2,1)} %param.28) | copy-start | bytes 393220
  9.8 51.5 %copy-start.9 = (bf16[128,256]{1,0:T(8,128)(2,1)S(1)}, bf16[128,256]{1,0:T(8,128)(2,1)}, u32[]{:S(2)}) copy-start(bf16[128,256]{1,0:T(8,128)(2,1)} %k_ref.1) | copy-start | bytes 196612
  9.8 51.6 %copy-start.10 = (bf16[128,256]{1,0:T(8,128)(2,1)S(1)}, bf16[128,256]{1,0:T(8,128)(2,1)}, u32[]{:S(2)}) copy-start(bf16[128,256]{1,0:T(8,128)(2,1)} %v_ref.1) | copy-start | bytes 196612

commit v2 on v1

v2 whole, which is shorter than its diff:
```python
import math

import jax
import jax.numpy as jnp
from jax import lax
from jax.experimental import pallas as pl
from jax.experimental.pallas import tpu as pltpu
from jax.sharding import PartitionSpec as P

HD = 128
NS = 16
BF = jnp.bfloat16
F32 = jnp.float32
MESH = pl.DeviceIdType.MESH
LOG2E = math.log2(math.e)
SCALE = LOG2E / math.sqrt(HD)
X_OFFSET = (0, 3, 1, 2)
GROUPS = ((0, 1), (1, 2), (3, 2), (5, 2), (7, 1))


def at(ctx, tp):
    return {"ctx": ctx, "tp": tp}


def remote(src, dst, send, recv, peer):
    return pltpu.make_async_remote_copy(
        src_ref=src, dst_ref=dst, send_sem=send, recv_sem=recv, device_id=peer, device_id_type=MESH
    )


def block_kernel(
    x_hbm, z_hbm, ck_hbm, cb_hbm, dd_hbm, sp_hbm, du_hbm, db_hbm, ld_hbm, sg_hbm,
    q_hbm, k_hbm, v_hbm, wt_hbm, res_hbm, mix_ref, out_ref,
    x_ref, z_ref, ck_ref, cb_ref, dd_ref, sp_ref, du_ref, db_ref, ld_ref, sg_ref,
    q_ref, k_ref, v_ref, res_ref,
    qts, vts, qt, kbuf, vtbuf, wbuf, m_ref, l_ref, acc, att, stage, landed, out_t,
    rim, padded, act, dpart, gpart, dland, gland, gsum, gates, steps, inject, scanned, decay,
    ends, total, ends_in, total_in, before, shift, column, column_in, entry_out, entry,
    load_sem, pair_send, pair_recv, kv_send, kv_recv, w_send, w_recv, half_send, half_recv,
    y_send, y_recv, rim_send, rim_recv, tp_send, tp_recv, col_send, col_recv, x_send, x_recv,
    back_send, back_recv,
):
    me = lax.axis_index("ctx")
    y = lax.axis_index("tp")
    core = me % 2
    other = 1 - core
    chip = me // 2
    z = chip % 8
    x = me // 16
    k = me % 16
    partner = at(me + 1 - 2 * core, y)
    after = at((me + 1) % 64, y)
    earlier = at((me + 63) % 64, y)
    right_z = at(x * 16 + ((z + 1) % 8) * 2 + core, y)
    left_z = at(x * 16 + ((z + 7) % 8) * 2 + core, y)
    right_x = at(((x + 1) % 4) * 16 + k, y)
    left_x = at(((x + 3) % 4) * 16 + k, y)

    def col_peer(gap):
        return at(x * 16 + (k + gap) % 16, y)

    def x_peer(gap):
        return at(((x + gap) % 4) * 16 + k, y)

    loads = {}
    pairs = (
        ("q", q_hbm, q_ref), ("k", k_hbm, k_ref), ("v", v_hbm, v_ref), ("w", wt_hbm, wbuf.at[0, 0]),
        ("x", x_hbm, x_ref), ("ck", ck_hbm, ck_ref), ("cb", cb_hbm, cb_ref), ("dd", dd_hbm, dd_ref),
        ("sp", sp_hbm, sp_ref), ("ld", ld_hbm, ld_ref), ("du", du_hbm, du_ref), ("db", db_hbm, db_ref),
        ("z", z_hbm, z_ref), ("sg", sg_hbm, sg_ref), ("res", res_hbm, res_ref),
    )
    for i, (name, src, dst) in enumerate(pairs):
        loads[name] = pltpu.make_async_copy(src, dst, load_sem.at[i])
        loads[name].start()

    barrier = pltpu.get_barrier_semaphore()

    def greet(peer):
        pl.semaphore_signal(barrier, inc=1, device_id=peer, device_id_type=MESH)

    greet(after)
    greet(earlier)
    for gap in (1, 2, 3):
        greet(x_peer(gap))
        for r in range(2):
            greet(at(chip * 2 + r, (y + gap) % 4))
    for gap in range(1, 16):
        greet(col_peer(gap))

    loads["q"].wait()
    for g in range(2):
        for h in range(4):
            head = q_ref[:, (g * 4 + h) * HD:(g * 4 + h + 1) * HD]
            qts[g, :, h * HD:(h + 1) * HD] = head.astype(F32).T.astype(BF)
    loads["k"].wait()
    loads["v"].wait()
    vts[...] = v_ref[...].astype(F32).T.astype(BF)
    loads["w"].wait()
    loads["x"].wait()
    pl.semaphore_wait(barrier, 26)

    own_rows = pl.ds(pl.multiple_of(core * 128, 128), 128)
    other_rows = pl.ds(pl.multiple_of(other * 128, 128), 128)
    own_cols = pl.ds(pl.multiple_of(core * 512, 512), 512)

    def pair_copy(src, dst, i):
        return remote(src, dst, pair_send.at[i], pair_recv.at[i], partner)

    swaps = (
        pair_copy(k_ref.at[:, other_rows], kbuf.at[0, 0, own_rows, :], 0),
        pair_copy(vts.at[other_rows, :], vtbuf.at[0, 0, :, own_rows], 1),
        pair_copy(qts.at[other], qt.at[:, own_cols], 2),
    )
    for swap in swaps:
        swap.start()
    rim_copy = remote(x_ref.at[pl.ds(112, 16), :], rim, rim_send.at[0], rim_recv.at[0], after)
    rim_copy.start()

    bufs = (kbuf, vtbuf)

    def kv_copy(kind, src, dst, peer):
        return remote(
            bufs[kind].at[src], bufs[kind].at[dst], kv_send.at[(kind, *dst)], kv_recv.at[(kind, *dst)], peer
        )

    def kv_arrived(kind, slot):
        kv_copy(kind, slot, slot, right_z).wait_recv()

    def spread_x(kind, zs):
        kv_copy(kind, (0, zs), (1, zs), right_x).start()
        kv_copy(kind, (0, zs), (2, zs), left_x).start()

    def w_copy(src, dst, peer):
        return remote(wbuf.at[src], wbuf.at[dst], w_send.at[dst], w_recv.at[dst], peer)

    def w_arrived(slot):
        w_copy(slot, slot, right_z).wait_recv()

    def half_copy(source, rows, i, peer):
        half = pl.ds(rows, 32)
        return remote(
            wbuf.at[0, source, half, :], wbuf.at[0, 3, half, :], half_send.at[i], half_recv.at[i], peer
        )

    def w_spread_z(xs):
        w_copy((0, xs), (1, xs), right_z).start()
        w_copy((0, xs), (2, xs), left_z).start()

    kbuf[0, 0, own_rows, :] = k_ref[:, own_rows]
    vtbuf[0, 0, :, own_rows] = vts[own_rows, :]
    qt[:, own_cols] = qts[core]
    for kind in (0, 1):
        swaps[kind].wait()
        kv_copy(kind, (0, 0), (0, 1), right_z).start()
        kv_copy(kind, (0, 0), (0, 2), left_z).start()
        spread_x(kind, 0)
    w_copy((0, 0), (0, 1), right_x).start()
    w_copy((0, 0), (0, 2), left_x).start()
    m_ref[...] = jnp.full_like(m_ref, -1e30)
    l_ref[...] = jnp.zeros_like(l_ref)
    acc[...] = jnp.zeros_like(acc)

    def kv_hop(h):
        for kind in (0, 1):
            if h < 4:
                kv_arrived(kind, (0, 2 * h - 1))
                if h < 3:
                    kv_copy(kind, (0, 2 * h - 1), (0, 2 * h + 1), right_z).start()
                elif kind == 0:
                    kv_copy(kind, (0, 5), (0, 7), right_z).start()
                spread_x(kind, 2 * h - 1)
                kv_arrived(kind, (0, 2 * h))
                if h < 3:
                    kv_copy(kind, (0, 2 * h), (0, 2 * h + 2), left_z).start()
                elif kind == 1:
                    kv_copy(kind, (0, 6), (0, 7), left_z).start()
                spread_x(kind, 2 * h)
            else:
                kv_arrived(kind, (0, 7))
                spread_x(kind, 7)

    loads["ck"].wait()
    loads["cb"].wait()
    padded[8:, :] = x_ref[...].astype(F32)
    rim_copy.wait()
    padded[:8, :] = jnp.where(me > 0, rim[8:, :].astype(F32), 0.0)
    for c in range(8):
        cols = slice(c * 256, (c + 1) * 256)
        conv = cb_ref[:, cols]
        for tap in range(4):
            conv = conv + ck_ref[tap:tap + 1, cols] * padded[5 + tap:133 + tap, cols]
        act[:, cols] = (conv / (1.0 + jnp.exp(-conv))).astype(BF)
    loads["dd"].wait()
    loads["sp"].wait()
    dpart[...] = jnp.dot(act[...], dd_ref[...], preferred_element_type=F32).astype(BF)
    gpart[...] = lax.dot_general(
        sp_ref[...], act[...], (((1,), (1,)), ((), ())), preferred_element_type=F32
    )

    def tp_copies(gap):
        peer = at(me, (y + gap) % 4)
        return (
            remote(dpart, dland.at[gap - 1], tp_send.at[0, gap], tp_recv.at[0, gap], peer),
            remote(gpart, gland.at[gap - 1], tp_send.at[1, gap], tp_recv.at[1, gap], peer),
        )

    for gap in (2, 1, 3):
        for copy in tp_copies(gap):
            copy.start()

    kv_hop(1)
    w_arrived((0, 1))
    half_copy(1, 0, 0, right_x).start()
    w_arrived((0, 2))
    half_copy(2, 32, 1, left_x).start()
    for xs in range(3):
        w_spread_z(xs)
    swaps[2].wait()

    def attend(slot, masked):
        for j in range(4):
            cols = pl.ds(j * 256, 256)
            s = jnp.dot(kbuf[slot], qt[:, cols], preferred_element_type=F32) * SCALE
            if masked:
                key = lax.broadcasted_iota(jnp.int32, (256, 256), 0)
                row = lax.broadcasted_iota(jnp.int32, (256, 256), 1) % 128 + (j // 2) * 128
                s = jnp.where(key <= row, s, -1e30)
            m_old = m_ref[:, cols]
            m_new = jnp.maximum(m_old, jnp.max(s, axis=0, keepdims=True))
            p = jnp.exp2(s - m_new)
            alpha = jnp.exp2(m_old - m_new)
            m_ref[:, cols] = m_new
            l_ref[:, cols] = l_ref[:, cols] * alpha + jnp.sum(p, axis=0, keepdims=True)
            acc[:, cols] = acc[:, cols] * alpha + jnp.dot(
                vtbuf[slot], p.astype(BF), preferred_element_type=F32
            )

    def z_of(zs):
        return (z + 8 + (1 - 2 * (zs % 2)) * ((zs + 1) // 2)) % 8

    def attend_earlier(xs, zs):
        source = ((x + X_OFFSET[xs]) % 4) * 8 + z_of(zs)

        @pl.when(source < chip)
        def _():
            attend((xs, zs), False)

    attend((0, 0), True)

    loads["ld"].wait()
    rate = -LOG2E * jnp.exp(ld_ref[...])
    for j in range(16):
        decay[pl.ds(j, 16, stride=16), :] = rate[:, j * 128:(j + 1) * 128]
    loads["du"].wait()
    loads["db"].wait()
    for gap in (1, 3, 2):
        for copy in tp_copies(gap):
            copy.wait()
    gsum[...] = gpart[...] + gland[0] + gland[1] + gland[2]
    to_scalars = pltpu.make_async_copy(gsum, gates, load_sem.at[0])
    to_scalars.start()
    low = (
        dpart[...].astype(F32) + dland[0].astype(F32) + dland[1].astype(F32) + dland[2].astype(F32)
    ).astype(BF)
    for c in range(8):
        cols = slice(c * 256, (c + 1) * 256)
        raw = jnp.dot(low, du_ref[:, cols], preferred_element_type=F32) + db_ref[:, cols]
        size = jnp.maximum(raw, 0.0) + jnp.log1p(jnp.exp(-jnp.abs(raw)))
        drive = size * act[:, cols].astype(F32)
        for half in range(2):
            j = c * 2 + half
            steps[pl.ds(j, 128, stride=16), :] = size[:, half * 128:(half + 1) * 128]
            inject[pl.ds(j, 128, stride=16), :] = drive[:, half * 128:(half + 1) * 128]
    kv_hop(2)
    half_copy(1, 0, 0, right_x).wait_recv()
    half_copy(2, 32, 1, left_x).wait_recv()
    w_spread_z(3)
    to_scalars.wait()

    def rows_of(t):
        return pl.ds(pl.multiple_of(t * 16, 16), 16)

    def first_pass(half):
        base = half * 8
        rates = [decay[(base + n) * 16:(base + n + 1) * 16, :] for n in range(8)]

        def advance(t, carried):
            size = steps[rows_of(t), :]
            drive = inject[rows_of(t), :]
            out = [
                jnp.exp2(rates[n] * size) * carried[n] + gates[base + n, t] * drive
                for n in range(8)
            ]
            return tuple(out) + (carried[8] + size,)

        zero = jnp.zeros((16, 128), F32)
        last = lax.fori_loop(0, 128, advance, (zero,) * 9, unroll=2)
        for n in range(8):
            ends[base + n] = last[n]
        if half == 0:
            total[...] = last[8]

    first_pass(0)
    kv_hop(3)
    first_pass(1)

    def col_copies(gap):
        peer = col_peer(gap)
        return (
            remote(ends.at[(k + gap) % 16], ends_in.at[gap], col_send.at[0, gap], col_recv.at[0, gap], peer),
            remote(total, total_in.at[gap], col_send.at[1, gap], col_recv.at[1, gap], peer),
        )

    def col_start(gap, _):
        for copy in col_copies(gap):
            copy.start()
        return 0

    def col_wait(gap, _):
        for copy in col_copies(gap):
            copy.wait()
        return 0

    lax.fori_loop(1, 16, col_start, 0)
    ends_in[0] = ends[k]
    total_in[0] = total[...]
    kv_hop(4)

    def x_copy(gap):
        return remote(column, column_in.at[gap - 1], x_send.at[gap], x_recv.at[gap], x_peer(gap))

    def column_stage():
        lax.fori_loop(1, 16, col_wait, 0)
        my_rate = decay[rows_of(k), :]

        def chain(j, carried):
            state, sizes = carried
            before[j] = state
            shift[j] = sizes
            slot = (k + 16 - j) % 16
            size = total_in[slot]
            return (jnp.exp2(my_rate * size) * state + ends_in[slot], sizes + size)

        zero = jnp.zeros((16, 128), F32)
        state, sizes = lax.fori_loop(0, 16, chain, (zero, zero))
        column[0] = state
        column[1] = sizes
        for gap in (2, 1, 3):
            x_copy(gap).start()

    def back_copy(gap):
        return remote(
            entry_out.at[(k + gap) % 16], entry.at[k], back_send.at[gap], back_recv.at[gap], col_peer(gap)
        )

    def back_arrival(gap):
        return remote(
            entry_out.at[(k + gap) % 16], entry.at[(k + 16 - gap) % 16],
            back_send.at[gap], back_recv.at[gap], col_peer(gap),
        )

    def back_start(gap, _):
        back_copy(gap).start()
        return 0

    def back_wait(gap, _):
        back_copy(gap).wait_send()
        back_arrival(gap).wait_recv()
        return 0

    def entry_stage():
        for gap in (1, 3, 2):
            x_copy(gap).wait()
        my_rate = decay[rows_of(k), :]
        incoming = jnp.zeros((16, 128), F32)
        for xs in range(3):
            slot = jnp.minimum((x + 3 - xs) % 4, 2)
            ahead = jnp.exp2(my_rate * column_in[slot, 1]) * incoming + column_in[slot, 0]
            incoming = jnp.where(xs < x, ahead, incoming)

        def finish(j, _):
            entry_out[j] = before[j] + jnp.exp2(my_rate * shift[j]) * incoming
            return 0

        lax.fori_loop(0, 16, finish, 0)
        lax.fori_loop(1, 16, back_start, 0)
        entry[k] = entry_out[k]

    def w_event(e):
        h = 1 + e // 4
        xs = e % 4
        w_arrived((2 * h - 1, xs))

        @pl.when((h < 3) | (xs < 2))
        def _():
            w_copy((2 * h - 1, xs), (2 * h + 1, xs), right_z).start()

        w_arrived((2 * h, xs))

        @pl.when(h < 3)
        def _():
            w_copy((2 * h, xs), (2 * h + 2, xs), left_z).start()

        @pl.when((h == 3) & (xs >= 2))
        def _():
            w_copy((2 * h, xs), (7, xs), left_z).start()

    def sweep(i, _):
        for kind in (0, 1):
            kv_arrived(kind, (1, i))

            @pl.when(i < 4)
            def _():
                kv_copy(kind, (1, i), (3, i), right_x).start()

            kv_arrived(kind, (2, i))

            @pl.when(i >= 4)
            def _():
                kv_copy(kind, (2, i), (3, i), left_x).start()

        w_event(i)

        @pl.when(i > 0)
        def _():
            attend_earlier(0, i)

        attend_earlier(1, i)
        attend_earlier(2, i)

        @pl.when(i > 0)
        def _():
            for kind in (0, 1):
                kv_arrived(kind, (3, i - 1))
            attend_earlier(3, i - 1)

        @pl.when(i == 2)
        def _():
            column_stage()

        @pl.when(i == 4)
        def _():
            entry_stage()

        return 0

    lax.fori_loop(0, 8, sweep, 0)
    for kind in (0, 1):
        kv_arrived(kind, (3, 7))
    attend_earlier(3, 7)

    inverse = 1.0 / l_ref[...]
    heads = []
    for h in range(4):
        pieces = []
        for r in range(2):
            cols = slice(r * 512 + h * 128, r * 512 + (h + 1) * 128)
            pieces.append((acc[:, cols] * inverse[:, cols]).astype(BF))
        heads.append(jnp.concatenate(pieces, axis=1))
    att[own_cols, :] = jnp.concatenate(heads, axis=0)
    att_swap = pair_copy(att.at[own_cols, :], att.at[own_cols, :], 3)
    att_swap.start()
    lax.fori_loop(1, 16, back_wait, 0)

    def second_pass(half):
        base = half * 8
        rates = [decay[(base + n) * 16:(base + n + 1) * 16, :] for n in range(8)]

        def advance(t, carried):
            size = steps[rows_of(t), :]
            drive = inject[rows_of(t), :]
            out = []
            mixed = scanned[rows_of(t), :] if half else None
            for n in range(8):
                state = jnp.exp2(rates[n] * size) * carried[n] + gates[base + n, t] * drive
                term = gates[NS + base + n, t] * state
                mixed = term if mixed is None else mixed + term
                out.append(state)
            scanned[rows_of(t), :] = mixed
            return tuple(out)

        lax.fori_loop(0, 128, advance, tuple(entry[base + n] for n in range(8)), unroll=2)

    def slot_of(gap):
        d = (y + gap + 4 - x) % 4
        return 2 * d - d // 2 - 4 * (d // 3)

    def y_copy(gap, r, g):
        first, count = GROUPS[g]
        rows = pl.ds(first, count)
        return remote(
            stage.at[slot_of(gap), r, rows], landed.at[gap, core, rows],
            y_send.at[gap, r, g], y_recv.at[gap, core, g], at(chip * 2 + r, (y + gap) % 4),
        )

    def y_arrival(gap, c, g):
        first, count = GROUPS[g]
        rows = pl.ds(first, count)
        return remote(
            stage.at[0, 0, rows], landed.at[gap, c, rows],
            y_send.at[gap, c, g], y_recv.at[gap, c, g], partner,
        )

    def project(g):
        first, count = GROUPS[g]
        for zs in range(first, first + count):
            part = jnp.dot(
                wbuf[zs].reshape(256, 1024), att[...], preferred_element_type=F32
            ).astype(BF)
            for xs in range(4):
                for r in range(2):
                    stage[xs, r, zs] = part[xs * 64:(xs + 1) * 64, r * 128:(r + 1) * 128]
        for gap in (2, 1, 3):
            for r in range(2):
                y_copy(gap, r, g).start()
        y_copy_partner(g).start()
        for zs in range(first, first + count):
            landed[0, core, zs] = stage[slot_of(0), core, zs]

    def y_copy_partner(g):
        first, count = GROUPS[g]
        rows = pl.ds(first, count)
        return remote(
            stage.at[slot_of(0), other, rows], landed.at[0, core, rows],
            y_send.at[0, 0, g], y_recv.at[0, core, g], partner,
        )

    second_pass(0)
    att_swap.wait()
    project(0)
    project(1)

    def late_event(e, _):
        w_event(e)
        return 0

    lax.fori_loop(8, 12, late_event, 0)
    project(2)
    second_pass(1)
    project(3)
    loads["z"].wait()
    loads["sg"].wait()
    for j in range(16):
        cols = slice(j * 128, (j + 1) * 128)
        gate = z_ref[:, cols].astype(F32)
        mixed = scanned[pl.ds(j, 128, stride=16), :] + sg_ref[:, cols] * act[:, cols].astype(F32)
        mix_ref[:, cols] = (mixed * (gate / (1.0 + jnp.exp(-gate)))).astype(BF)
    for xs in range(4):
        w_arrived((7, xs))
    project(4)

    loads["res"].wait()
    for g in range(5):
        y_arrival(0, other, g).wait_recv()
        for gap in (1, 3, 2):
            for c in range(2):
                y_arrival(gap, c, g).wait_recv()
        first, count = GROUPS[g]
        for zs in range(first, first + count):
            for c in range(2):
                part = landed[0, c, zs].astype(F32)
                for gap in range(1, 4):
                    part = part + landed[gap, c, zs].astype(F32)
                rows = pl.ds(pl.multiple_of(z_of(zs) * 128 + c * 64, 64), 64)
                out_t[rows, :] = part
    for zo in range(8):
        cols = slice(zo * 128, (zo + 1) * 128)
        out_ref[:, cols] = (res_ref[:, cols].astype(F32) + out_t[cols, :].T).astype(BF)

    for g in range(5):
        y_copy_partner(g).wait_send()
        for gap in (1, 2, 3):
            for r in range(2):
                y_copy(gap, r, g).wait_send()
    for i in range(2):
        half_copy(i + 1, 32 * i, i, right_x).wait_send()
    w_copy((0, 0), (0, 1), right_x).wait_send()
    w_copy((0, 0), (0, 2), left_x).wait_send()

    def drain(zs, _):
        for kind in (0, 1):
            @pl.when((zs > 0) & (zs < 7))
            def _():
                kv_copy(kind, (0, zs), (0, zs), right_z).wait_send()

            for xs in range(1, 4):
                kv_copy(kind, (xs, zs), (xs, zs), right_z).wait_send()

        @pl.when(zs > 0)
        def _():
            for xs in range(4):
                w_copy((zs, xs), (zs, xs), right_z).wait_send()

        return 0

    lax.fori_loop(0, 8, drain, 0)
    for kind in (0, 1):
        kv_copy(kind, (0, 7), (0, 7), right_z).wait_send()


def block(
    x_stream, z_stream, conv_kernel, conv_bias, delta_down, state_proj, delta_up, delta_bias,
    log_decay, skip_gain, queries, key_heads, values, out_proj, residual,
):
    dma = pltpu.SemaphoreType.DMA
    operands = (
        x_stream, z_stream, conv_kernel, conv_bias[None, :], delta_down, state_proj, delta_up,
        delta_bias[None, :], log_decay, skip_gain[None, :], queries, key_heads, values, out_proj.T, residual,
    )
    copies = [pltpu.VMEM(a.shape, a.dtype) for i, a in enumerate(operands) if i != 13]
    states = pltpu.VMEM((16, 16, 128), F32)
    by_token = pltpu.VMEM((2048, 128), F32)
    return pl.pallas_call(
        block_kernel,
        out_shape=(
            jax.ShapeDtypeStruct(x_stream.shape, BF), jax.ShapeDtypeStruct(residual.shape, BF)
        ),
        in_specs=[pl.BlockSpec(memory_space=pl.ANY)] * 15,
        out_specs=(pl.BlockSpec(memory_space=pltpu.VMEM),) * 2,
        scratch_shapes=copies + [
            pltpu.VMEM((2, 128, 512), BF),
            pltpu.VMEM((256, 128), BF),
            pltpu.VMEM((128, 1024), BF),
            pltpu.VMEM((4, 8, 256, 128), BF),
            pltpu.VMEM((4, 8, 128, 256), BF),
            pltpu.VMEM((8, 4, 64, 1024), BF),
            pltpu.VMEM((1, 1024), F32),
            pltpu.VMEM((1, 1024), F32),
            pltpu.VMEM((128, 1024), F32),
            pltpu.VMEM((1024, 256), BF),
            pltpu.VMEM((4, 2, 8, 64, 128), BF),
            pltpu.VMEM((4, 2, 8, 64, 128), BF),
            pltpu.VMEM((1024, 128), F32),
            pltpu.VMEM((16, 2048), BF),
            pltpu.VMEM((136, 2048), F32),
            pltpu.VMEM((128, 2048), BF),
            pltpu.VMEM((128, 256), BF),
            pltpu.VMEM((32, 128), F32),
            pltpu.VMEM((3, 128, 256), BF),
            pltpu.VMEM((3, 32, 128), F32),
            pltpu.VMEM((32, 128), F32),
            pltpu.SMEM((32, 128), F32),
            by_token, by_token, by_token,
            pltpu.VMEM((256, 128), F32),
            states,
            pltpu.VMEM((16, 128), F32),
            states, states, states, states,
            pltpu.VMEM((2, 16, 128), F32),
            pltpu.VMEM((3, 2, 16, 128), F32),
            states, states,
            dma((15,)), dma((4,)), dma((4,)), dma((2, 4, 8)), dma((2, 4, 8)), dma((8, 4)), dma((8, 4)),
            dma((2,)), dma((2,)), dma((4, 2, 5)), dma((4, 2, 5)), dma((1,)), dma((1,)),
            dma((2, 4)), dma((2, 4)), dma((2, 16)), dma((2, 16)), dma((4,)), dma((4,)),
            dma((16,)), dma((16,)),
        ],
        compiler_params=pltpu.CompilerParams(
            collective_id=0, has_side_effects=True, vmem_limit_bytes=56 * 1024 * 1024
        ),
    )(*operands)


def solution(mesh):
    both = P("ctx", "tp")
    placed = (
        both, both, P(None, "tp"), P("tp"), P("tp", None), P(None, "tp"), P(None, "tp"), P("tp"),
        P(None, "tp"), P("tp"), both, both, both, P("tp", "ctx"), both,
    )
    return jax.shard_map(
        block, mesh=mesh, in_specs=placed, out_specs=(both, both), check_vma=False
    )
```

time: 162 us -> 102 us (0.63)
  the two profiles are of different devices: /device:TPU:1 before, /device:TPU:7 now
where the time goes in v2:
time: 102 us
  Pallas kernels  98.6 us (97%)
  local copies, waits for them, and re-layouts  2.63 us (3%)
    pallas_call x1, Pallas kernels, block(): pl.pallas_call(block_kernel, out_shape=(jax.ShapeDtypeStruct(x_stream.sha...  98.6 us
    unnamed x4, local copies, waits for them, and re-layouts  2.63 us

profile of v2, /device:TPU:7, one launch (start us, length us, event | category | flops | bytes accessed | tf_op | source)
XLA Modules:
  0.0 101.9 jit_solution(14272883608377753474)
XLA Ops:
  0.6 98.6 %shard_map.158 = (bf16[128,2048]{1,0:T(8,128)(2,1)}, bf16[128,1024]{1,0:T(8,128)(2,1)}) custom-call(bf16[128,2048]{1,0:T(8,128)(2,1)} %x_hbm.1, bf16[128,2048]{1,0:T(8,128)(2,1)} %z_hbm.1, f32[4,2048]{1,0:T(4,128)} %ck_hbm.1, f32[1,2048]{1,0:T(1,128)} %bitcast.5, bf16[2048,256]{1,0:T(8,128)(2,1)} %dd_hbm.1, bf16[32,2048]{1,0:T(8,128)(2,1)} %sp_hbm.1, ...), custom_call_target="tpu_custom_call" | custom-call | tf_op jit(solution)/shard_map/pallas_call | solution.py:613
  99.3 0.0 copy-start
  99.3 1.9 %copy.19 = bf16[128,2048]{1,0:T(8,128)(2,1)} copy(bf16[128,2048]{1,0:T(8,128)(2,1)} %get-tuple-element.4) | data formatting | bytes 1048576
  101.2 0.0 copy-done
  101.2 0.7 copy.20
Async XLA Ops:
  99.3 1.9 %copy-start = (bf16[128,1024]{1,0:T(8,128)(2,1)S(1)}, bf16[128,1024]{1,0:T(8,128)(2,1)}, u32[]{:S(2)}) copy-start(bf16[128,1024]{1,0:T(8,128)(2,1)} %get-tuple-element.5) | copy-start | bytes 786436

commit v3 on v2

--- a/solution.py
+++ b/solution.py
@@ -15,6 +15,8 @@
 LOG2E = math.log2(math.e)
 SCALE = LOG2E / math.sqrt(HD)
 X_OFFSET = (0, 3, 1, 2)
+WIDE = 512
+LOW = 16
 GROUPS = ((0, 1), (1, 2), (3, 2), (5, 2), (7, 1))
 
 
@@ -33,9 +35,9 @@
     q_hbm, k_hbm, v_hbm, wt_hbm, res_hbm, mix_ref, out_ref,
     x_ref, z_ref, ck_ref, cb_ref, dd_ref, sp_ref, du_ref, db_ref, ld_ref, sg_ref,
     q_ref, k_ref, v_ref, res_ref,
-    qts, vts, qt, kbuf, vtbuf, wbuf, m_ref, l_ref, acc, att, stage, landed, out_t,
+    qts, vts, qt, kbuf, vtbuf, wlow, wbuf, m_ref, l_ref, acc, att, stage, landed, stage_low, landed_low, out_t,
     rim, padded, act, dpart, gpart, dland, gland, gsum, gates, steps, inject, scanned, decay,
-    ends, total, ends_in, total_in, before, shift, column, column_in, entry_out, entry,
+    ends, ends_in, before, shift, column, column_in, entry_out, entry,
     load_sem, pair_send, pair_recv, kv_send, kv_recv, w_send, w_recv, half_send, half_recv,
     y_send, y_recv, rim_send, rim_recv, tp_send, tp_recv, col_send, col_recv, x_send, x_recv,
     back_send, back_recv,
@@ -62,17 +64,6 @@
     def x_peer(gap):
         return at(((x + gap) % 4) * 16 + k, y)
 
-    loads = {}
-    pairs = (
-        ("q", q_hbm, q_ref), ("k", k_hbm, k_ref), ("v", v_hbm, v_ref), ("w", wt_hbm, wbuf.at[0, 0]),
-        ("x", x_hbm, x_ref), ("ck", ck_hbm, ck_ref), ("cb", cb_hbm, cb_ref), ("dd", dd_hbm, dd_ref),
-        ("sp", sp_hbm, sp_ref), ("ld", ld_hbm, ld_ref), ("du", du_hbm, du_ref), ("db", db_hbm, db_ref),
-        ("z", z_hbm, z_ref), ("sg", sg_hbm, sg_ref), ("res", res_hbm, res_ref),
-    )
-    for i, (name, src, dst) in enumerate(pairs):
-        loads[name] = pltpu.make_async_copy(src, dst, load_sem.at[i])
-        loads[name].start()
-
     barrier = pltpu.get_barrier_semaphore()
 
     def greet(peer):
@@ -87,16 +78,49 @@
     for gap in range(1, 16):
         greet(col_peer(gap))
 
+    loads = {}
+    pairs = (
+        ("v", v_hbm, v_ref), ("k", k_hbm, k_ref), ("w", wt_hbm.at[pl.ds(LOW, 64 - LOW)], wbuf.at[0, 0]), ("wl", wt_hbm.at[pl.ds(0, LOW)], wlow.at[0, 0]), ("q", q_hbm, q_ref),
+        ("x", x_hbm, x_ref), ("ck", ck_hbm, ck_ref), ("cb", cb_hbm, cb_ref), ("dd", dd_hbm, dd_ref),
+        ("sp", sp_hbm, sp_ref), ("ld", ld_hbm, ld_ref), ("du", du_hbm, du_ref), ("db", db_hbm, db_ref),
+        ("z", z_hbm, z_ref), ("sg", sg_hbm, sg_ref), ("res", res_hbm, res_ref),
+    )
+    for i, (name, src, dst) in enumerate(pairs):
+        loads[name] = pltpu.make_async_copy(src, dst, load_sem.at[i])
+        loads[name].start()
+
+    loads["v"].wait()
+    vts[...] = v_ref[...].astype(F32).T.astype(BF)
     loads["q"].wait()
     for g in range(2):
         for h in range(4):
             head = q_ref[:, (g * 4 + h) * HD:(g * 4 + h + 1) * HD]
             qts[g, :, h * HD:(h + 1) * HD] = head.astype(F32).T.astype(BF)
+    m_ref[...] = jnp.full_like(m_ref, -1e30)
+    l_ref[...] = jnp.zeros_like(l_ref)
+    acc[...] = jnp.zeros_like(acc)
+
+    def convolve(count):
+        for c in range(8):
+            cols = slice(c * 256, (c + 1) * 256)
+            conv = cb_ref[:, cols]
+            for tap in range(4):
+                conv = conv + ck_ref[tap:tap + 1, cols] * padded[5 + tap:5 + tap + count, cols]
+            act[:count, cols] = (conv / (1.0 + jnp.exp(-conv))).astype(BF)
+
+    loads["x"].wait()
+    loads["ck"].wait()
+    loads["cb"].wait()
+    padded[:8, :] = jnp.zeros((8, 2048), F32)
+    padded[8:, :] = x_ref[...].astype(F32)
+    convolve(128)
+    loads["ld"].wait()
+    rate = -LOG2E * jnp.exp(ld_ref[...])
+    for j in range(16):
+        decay[pl.ds(j, 16, stride=16), :] = rate[:, j * 128:(j + 1) * 128]
     loads["k"].wait()
-    loads["v"].wait()
-    vts[...] = v_ref[...].astype(F32).T.astype(BF)
     loads["w"].wait()
-    loads["x"].wait()
+    loads["wl"].wait()
     pl.semaphore_wait(barrier, 26)
 
     own_rows = pl.ds(pl.multiple_of(core * 128, 128), 128)
@@ -113,10 +137,8 @@
     )
     for swap in swaps:
         swap.start()
-    rim_copy = remote(x_ref.at[pl.ds(112, 16), :], rim, rim_send.at[0], rim_recv.at[0], after)
-    rim_copy.start()
-
-    bufs = (kbuf, vtbuf)
+
+    bufs = (kbuf, vtbuf, wlow)
 
     def kv_copy(kind, src, dst, peer):
         return remote(
@@ -137,7 +159,7 @@
         w_copy(slot, slot, right_z).wait_recv()
 
     def half_copy(source, rows, i, peer):
-        half = pl.ds(rows, 32)
+        half = pl.ds(rows, 32 - rows // 2)
         return remote(
             wbuf.at[0, source, half, :], wbuf.at[0, 3, half, :], half_send.at[i], half_recv.at[i], peer
         )
@@ -146,19 +168,32 @@
         w_copy((0, xs), (1, xs), right_z).start()
         w_copy((0, xs), (2, xs), left_z).start()
 
+    w_copy((0, 0), (0, 1), right_x).start()
+    w_copy((0, 0), (0, 2), left_x).start()
     kbuf[0, 0, own_rows, :] = k_ref[:, own_rows]
     vtbuf[0, 0, :, own_rows] = vts[own_rows, :]
+    rim_copy = remote(x_ref.at[pl.ds(112, 16), :], rim, rim_send.at[0], rim_recv.at[0], after)
+    rim_copy.start()
     qt[:, own_cols] = qts[core]
     for kind in (0, 1):
         swaps[kind].wait()
         kv_copy(kind, (0, 0), (0, 1), right_z).start()
         kv_copy(kind, (0, 0), (0, 2), left_z).start()
         spread_x(kind, 0)
-    w_copy((0, 0), (0, 1), right_x).start()
-    w_copy((0, 0), (0, 2), left_x).start()
-    m_ref[...] = jnp.full_like(m_ref, -1e30)
-    l_ref[...] = jnp.zeros_like(l_ref)
-    acc[...] = jnp.zeros_like(acc)
+    w_spread_z(0)
+
+    def low_hop(h):
+        if h == 0:
+            kv_copy(2, (0, 0), (0, 1), right_z).start()
+            kv_copy(2, (0, 0), (0, 2), left_z).start()
+        elif h < 4:
+            kv_arrived(2, (0, 2 * h - 1))
+            kv_copy(2, (0, 2 * h - 1), (0, 2 * h + 1), right_z).start()
+            kv_arrived(2, (0, 2 * h))
+            if h < 3:
+                kv_copy(2, (0, 2 * h), (0, 2 * h + 2), left_z).start()
+        else:
+            kv_arrived(2, (0, 7))
 
     def kv_hop(h):
         for kind in (0, 1):
@@ -179,17 +214,56 @@
                 kv_arrived(kind, (0, 7))
                 spread_x(kind, 7)
 
-    loads["ck"].wait()
-    loads["cb"].wait()
-    padded[8:, :] = x_ref[...].astype(F32)
+    def attend(slots, biases):
+        def scores(j):
+            cols = slice(j * WIDE, (j + 1) * WIDE)
+            return [jnp.dot(kbuf[slot], qt[:, cols], preferred_element_type=F32) for slot in slots]
+
+        following = scores(0)
+        for j in range(1024 // WIDE):
+            cols = slice(j * WIDE, (j + 1) * WIDE)
+            now = following
+            if (j + 1) * WIDE < 1024:
+                following = scores(j + 1)
+            if biases is None:
+                key = lax.broadcasted_iota(jnp.int32, (256, WIDE), 0)
+                row = lax.broadcasted_iota(jnp.int32, (256, WIDE), 1) % 128 + (j * WIDE // 512) * 128
+                now = [jnp.where(key <= row, s, -1e30) for s in now]
+            m_old = m_ref[:, cols]
+            m_new = m_old
+            for i, s in enumerate(now):
+                top = jnp.max(s, axis=0, keepdims=True) * SCALE
+                m_new = jnp.maximum(m_new, top if biases is None else top + biases[i])
+            alpha = jnp.exp2(m_old - m_new)
+            gained = l_ref[:, cols] * alpha
+            mixed = acc[:, cols] * alpha
+            for i, s in enumerate(now):
+                p = jnp.exp2(s * SCALE - (m_new if biases is None else m_new - biases[i]))
+                gained = gained + jnp.sum(p, axis=0, keepdims=True)
+                mixed = mixed + jnp.dot(vtbuf[slots[i]], p.astype(BF), preferred_element_type=F32)
+            m_ref[:, cols] = m_new
+            l_ref[:, cols] = gained
+            acc[:, cols] = mixed
+
+    def z_of(zs):
+        return (z + 8 + (1 - 2 * (zs % 2)) * ((zs + 1) // 2)) % 8
+
+    def attend_earlier(first, second, zs):
+        earlier_than = [((x + X_OFFSET[xs]) % 4) * 8 + z_of(zs) < chip for xs in (first, second)]
+
+        @pl.when(earlier_than[0] | earlier_than[1])
+        def _():
+            attend(
+                [(xs, zs) for xs in (first, second)],
+                [jnp.where(flag, 0.0, -1e30).astype(F32) for flag in earlier_than],
+            )
+
+    swaps[2].wait()
+    attend([(0, 0)], None)
+
     rim_copy.wait()
     padded[:8, :] = jnp.where(me > 0, rim[8:, :].astype(F32), 0.0)
-    for c in range(8):
-        cols = slice(c * 256, (c + 1) * 256)
-        conv = cb_ref[:, cols]
-        for tap in range(4):
-            conv = conv + ck_ref[tap:tap + 1, cols] * padded[5 + tap:133 + tap, cols]
-        act[:, cols] = (conv / (1.0 + jnp.exp(-conv))).astype(BF)
+    convolve(16)
     loads["dd"].wait()
     loads["sp"].wait()
     dpart[...] = jnp.dot(act[...], dd_ref[...], preferred_element_type=F32).astype(BF)
@@ -208,74 +282,37 @@
         for copy in tp_copies(gap):
             copy.start()
 
+
     kv_hop(1)
     w_arrived((0, 1))
     half_copy(1, 0, 0, right_x).start()
     w_arrived((0, 2))
     half_copy(2, 32, 1, left_x).start()
-    for xs in range(3):
-        w_spread_z(xs)
-    swaps[2].wait()
-
-    def attend(slot, masked):
-        for j in range(4):
-            cols = pl.ds(j * 256, 256)
-            s = jnp.dot(kbuf[slot], qt[:, cols], preferred_element_type=F32) * SCALE
-            if masked:
-                key = lax.broadcasted_iota(jnp.int32, (256, 256), 0)
-                row = lax.broadcasted_iota(jnp.int32, (256, 256), 1) % 128 + (j // 2) * 128
-                s = jnp.where(key <= row, s, -1e30)
-            m_old = m_ref[:, cols]
-            m_new = jnp.maximum(m_old, jnp.max(s, axis=0, keepdims=True))
-            p = jnp.exp2(s - m_new)
-            alpha = jnp.exp2(m_old - m_new)
-            m_ref[:, cols] = m_new
-            l_ref[:, cols] = l_ref[:, cols] * alpha + jnp.sum(p, axis=0, keepdims=True)
-            acc[:, cols] = acc[:, cols] * alpha + jnp.dot(
-                vtbuf[slot], p.astype(BF), preferred_element_type=F32
-            )
-
-    def z_of(zs):
-        return (z + 8 + (1 - 2 * (zs % 2)) * ((zs + 1) // 2)) % 8
-
-    def attend_earlier(xs, zs):
-        source = ((x + X_OFFSET[xs]) % 4) * 8 + z_of(zs)
-
-        @pl.when(source < chip)
-        def _():
-            attend((xs, zs), False)
-
-    attend((0, 0), True)
-
-    loads["ld"].wait()
-    rate = -LOG2E * jnp.exp(ld_ref[...])
-    for j in range(16):
-        decay[pl.ds(j, 16, stride=16), :] = rate[:, j * 128:(j + 1) * 128]
-    loads["du"].wait()
-    loads["db"].wait()
-    for gap in (1, 3, 2):
-        for copy in tp_copies(gap):
-            copy.wait()
-    gsum[...] = gpart[...] + gland[0] + gland[1] + gland[2]
-    to_scalars = pltpu.make_async_copy(gsum, gates, load_sem.at[0])
-    to_scalars.start()
-    low = (
-        dpart[...].astype(F32) + dland[0].astype(F32) + dland[1].astype(F32) + dland[2].astype(F32)
-    ).astype(BF)
-    for c in range(8):
-        cols = slice(c * 256, (c + 1) * 256)
-        raw = jnp.dot(low, du_ref[:, cols], preferred_element_type=F32) + db_ref[:, cols]
-        size = jnp.maximum(raw, 0.0) + jnp.log1p(jnp.exp(-jnp.abs(raw)))
-        drive = size * act[:, cols].astype(F32)
-        for half in range(2):
-            j = c * 2 + half
-            steps[pl.ds(j, 128, stride=16), :] = size[:, half * 128:(half + 1) * 128]
-            inject[pl.ds(j, 128, stride=16), :] = drive[:, half * 128:(half + 1) * 128]
-    kv_hop(2)
-    half_copy(1, 0, 0, right_x).wait_recv()
-    half_copy(2, 32, 1, left_x).wait_recv()
-    w_spread_z(3)
-    to_scalars.wait()
+    w_spread_z(1)
+    low_hop(0)
+
+    def step_stage():
+        loads["du"].wait()
+        loads["db"].wait()
+        for gap in (1, 3, 2):
+            for copy in tp_copies(gap):
+                copy.wait()
+        gsum[...] = gpart[...] + gland[0] + gland[1] + gland[2]
+        to_scalars = pltpu.make_async_copy(gsum, gates, load_sem.at[0])
+        to_scalars.start()
+        low = (
+            dpart[...].astype(F32) + dland[0].astype(F32) + dland[1].astype(F32) + dland[2].astype(F32)
+        ).astype(BF)
+        for c in range(8):
+            cols = slice(c * 256, (c + 1) * 256)
+            raw = jnp.dot(low, du_ref[:, cols], preferred_element_type=F32) + db_ref[:, cols]
+            size = jnp.maximum(raw, 0.0) + jnp.log1p(jnp.exp(-jnp.abs(raw)))
+            drive = size * act[:, cols].astype(F32)
+            for half in range(2):
+                j = c * 2 + half
+                steps[pl.ds(j, 128, stride=16), :] = size[:, half * 128:(half + 1) * 128]
+                inject[pl.ds(j, 128, stride=16), :] = drive[:, half * 128:(half + 1) * 128]
+        to_scalars.wait()
 
     def rows_of(t):
         return pl.ds(pl.multiple_of(t * 16, 16), 16)
@@ -296,19 +333,13 @@
         zero = jnp.zeros((16, 128), F32)
         last = lax.fori_loop(0, 128, advance, (zero,) * 9, unroll=2)
         for n in range(8):
-            ends[base + n] = last[n]
-        if half == 0:
-            total[...] = last[8]
-
-    first_pass(0)
-    kv_hop(3)
-    first_pass(1)
+            ends[base + n, 0] = last[n].astype(BF)
+            ends[base + n, 1] = last[8].astype(BF)
 
     def col_copies(gap):
         peer = col_peer(gap)
         return (
-            remote(ends.at[(k + gap) % 16], ends_in.at[gap], col_send.at[0, gap], col_recv.at[0, gap], peer),
-            remote(total, total_in.at[gap], col_send.at[1, gap], col_recv.at[1, gap], peer),
+            remote(ends.at[(k + gap) % 16], ends_in.at[gap], col_send.at[gap], col_recv.at[gap], peer),
         )
 
     def col_start(gap, _):
@@ -321,10 +352,9 @@
             copy.wait()
         return 0
 
-    lax.fori_loop(1, 16, col_start, 0)
-    ends_in[0] = ends[k]
-    total_in[0] = total[...]
-    kv_hop(4)
+    def ends_stage():
+        lax.fori_loop(1, 16, col_start, 0)
+        ends_in[0] = ends[k]
 
     def x_copy(gap):
         return remote(column, column_in.at[gap - 1], x_send.at[gap], x_recv.at[gap], x_peer(gap))
@@ -338,8 +368,8 @@
             before[j] = state
             shift[j] = sizes
             slot = (k + 16 - j) % 16
-            size = total_in[slot]
-            return (jnp.exp2(my_rate * size) * state + ends_in[slot], sizes + size)
+            size = ends_in[slot, 1].astype(F32)
+            return (jnp.exp2(my_rate * size) * state + ends_in[slot, 0].astype(F32), sizes + size)
 
         zero = jnp.zeros((16, 128), F32)
         state, sizes = lax.fori_loop(0, 16, chain, (zero, zero))
@@ -379,7 +409,7 @@
             incoming = jnp.where(xs < x, ahead, incoming)
 
         def finish(j, _):
-            entry_out[j] = before[j] + jnp.exp2(my_rate * shift[j]) * incoming
+            entry_out[j] = (before[j] + jnp.exp2(my_rate * shift[j]) * incoming).astype(BF)
             return 0
 
         lax.fori_loop(0, 16, finish, 0)
@@ -406,39 +436,64 @@
             w_copy((2 * h, xs), (7, xs), left_z).start()
 
     def sweep(i, _):
-        for kind in (0, 1):
+        @pl.when(i == 1)
+        def _():
+            kv_hop(2)
+            low_hop(1)
+            w_spread_z(2)
+
+        @pl.when(i == 2)
+        def _():
+            kv_hop(3)
+            low_hop(2)
+            half_copy(1, 0, 0, right_x).wait_recv()
+            half_copy(2, 32, 1, left_x).wait_recv()
+            w_spread_z(3)
+
+        @pl.when(i == 3)
+        def _():
+            kv_hop(4)
+            low_hop(3)
+
+        for kind, near, peer in ((0, 1, right_x), (1, 2, left_x)):
             kv_arrived(kind, (1, i))
-
-            @pl.when(i < 4)
-            def _():
-                kv_copy(kind, (1, i), (3, i), right_x).start()
-
             kv_arrived(kind, (2, i))
-
-            @pl.when(i >= 4)
-            def _():
-                kv_copy(kind, (2, i), (3, i), left_x).start()
-
-        w_event(i)
-
-        @pl.when(i > 0)
-        def _():
-            attend_earlier(0, i)
-
-        attend_earlier(1, i)
-        attend_earlier(2, i)
+            kv_copy(kind, (near, i), (3, i), peer).start()
+
+        @pl.when(i >= 2)
+        def _():
+            w_event(i - 2 + i // 7)
+
+        attend_earlier(1, 2, i)
+
+        @pl.when(i == 6)
+        def _():
+            w_event(5)
+
+        @pl.when(i == 0)
+        def _():
+            step_stage()
+
+        @pl.when(i == 1)
+        def _():
+            first_pass(0)
+
+        @pl.when(i == 2)
+        def _():
+            first_pass(1)
+            ends_stage()
 
         @pl.when(i > 0)
         def _():
             for kind in (0, 1):
                 kv_arrived(kind, (3, i - 1))
-            attend_earlier(3, i - 1)
-
-        @pl.when(i == 2)
+            attend_earlier(0, 3, i - 1)
+
+        @pl.when(i == 4)
         def _():
             column_stage()
 
-        @pl.when(i == 4)
+        @pl.when(i == 6)
         def _():
             entry_stage()
 
@@ -447,8 +502,15 @@
     lax.fori_loop(0, 8, sweep, 0)
     for kind in (0, 1):
         kv_arrived(kind, (3, 7))
-    attend_earlier(3, 7)
-
+    attend_earlier(0, 3, 7)
+
+    low_hop(4)
+
+    def low_spread(zs, _):
+        spread_x(2, zs)
+        return 0
+
+    lax.fori_loop(0, 8, low_spread, 0)
     inverse = 1.0 / l_ref[...]
     heads = []
     for h in range(4):
@@ -479,7 +541,7 @@
             scanned[rows_of(t), :] = mixed
             return tuple(out)
 
-        lax.fori_loop(0, 128, advance, tuple(entry[base + n] for n in range(8)), unroll=2)
+        lax.fori_loop(0, 128, advance, tuple(entry[base + n].astype(F32) for n in range(8)), unroll=2)
 
     def slot_of(gap):
         d = (y + gap + 4 - x) % 4
@@ -505,11 +567,11 @@
         first, count = GROUPS[g]
         for zs in range(first, first + count):
             part = jnp.dot(
-                wbuf[zs].reshape(256, 1024), att[...], preferred_element_type=F32
+                wbuf[zs].reshape(4 * (64 - LOW), 1024), att[...], preferred_element_type=F32
             ).astype(BF)
             for xs in range(4):
                 for r in range(2):
-                    stage[xs, r, zs] = part[xs * 64:(xs + 1) * 64, r * 128:(r + 1) * 128]
+                    stage[xs, r, zs] = part[xs * (64 - LOW):(xs + 1) * (64 - LOW), r * 128:(r + 1) * 128]
         for gap in (2, 1, 3):
             for r in range(2):
                 y_copy(gap, r, g).start()
@@ -525,17 +587,56 @@
             y_send.at[0, 0, g], y_recv.at[0, core, g], partner,
         )
 
-    second_pass(0)
+    def low_cross(i, _):
+        for zs, near, peer in ((2 * i, 1, right_x), (2 * i + 1, 2, left_x)):
+            kv_arrived(2, (1, zs))
+            kv_arrived(2, (2, zs))
+            kv_copy(2, (near, zs), (3, zs), peer).start()
+        return 0
+
+    def y_low(gap, r):
+        return remote(
+            stage_low.at[slot_of(gap), r], landed_low.at[gap, core],
+            y_send.at[gap, r, 5], y_recv.at[gap, core, 5], at(chip * 2 + r, (y + gap) % 4),
+        )
+
+    def y_low_partner():
+        return remote(
+            stage_low.at[slot_of(0), other], landed_low.at[0, core],
+            y_send.at[0, 0, 5], y_recv.at[0, core, 5], partner,
+        )
+
+    def y_low_arrival(gap, c):
+        return remote(
+            stage_low.at[0, 0], landed_low.at[gap, c], y_send.at[gap, c, 5], y_recv.at[gap, c, 5], partner
+        )
+
+    def project_low():
+        for zs in range(8):
+            kv_arrived(2, (3, zs))
+        for xs in range(4):
+            part = jnp.dot(
+                wlow[xs].reshape(8 * LOW, 1024), att[...], preferred_element_type=F32
+            ).astype(BF)
+            for r in range(2):
+                stage_low[xs, r] = part[:, r * 128:(r + 1) * 128].reshape(8, LOW, 128)
+        for gap in (2, 1, 3):
+            for r in range(2):
+                y_low(gap, r).start()
+        y_low_partner().start()
+        landed_low[0, core] = stage_low[slot_of(0), core]
+
+    w_event(7)
     att_swap.wait()
     project(0)
     project(1)
-
-    def late_event(e, _):
-        w_event(e)
-        return 0
-
-    lax.fori_loop(8, 12, late_event, 0)
     project(2)
+    w_event(8)
+    w_event(9)
+    lax.fori_loop(0, 4, low_cross, 0)
+    second_pass(0)
+    w_event(10)
+    w_event(11)
     second_pass(1)
     project(3)
     loads["z"].wait()
@@ -545,6 +646,7 @@
         gate = z_ref[:, cols].astype(F32)
         mixed = scanned[pl.ds(j, 128, stride=16), :] + sg_ref[:, cols] * act[:, cols].astype(F32)
         mix_ref[:, cols] = (mixed * (gate / (1.0 + jnp.exp(-gate)))).astype(BF)
+    project_low()
     for xs in range(4):
         w_arrived((7, xs))
     project(4)
@@ -561,8 +663,19 @@
                 part = landed[0, c, zs].astype(F32)
                 for gap in range(1, 4):
                     part = part + landed[gap, c, zs].astype(F32)
-                rows = pl.ds(pl.multiple_of(z_of(zs) * 128 + c * 64, 64), 64)
+                rows = pl.ds(pl.multiple_of(z_of(zs) * 128 + c * 64 + LOW, LOW), 64 - LOW)
                 out_t[rows, :] = part
+    y_low_arrival(0, other).wait_recv()
+    for gap in (1, 3, 2):
+        for c in range(2):
+            y_low_arrival(gap, c).wait_recv()
+    for zs in range(8):
+        for c in range(2):
+            part = landed_low[0, c, zs].astype(F32)
+            for gap in range(1, 4):
+                part = part + landed_low[gap, c, zs].astype(F32)
+            rows = pl.ds(pl.multiple_of(z_of(zs) * 128 + c * 64, 64), LOW)
+            out_t[rows, :] = part
     for zo in range(8):
         cols = slice(zo * 128, (zo + 1) * 128)
         out_ref[:, cols] = (res_ref[:, cols].astype(F32) + out_t[cols, :].T).astype(BF)
@@ -572,13 +685,17 @@
         for gap in (1, 2, 3):
             for r in range(2):
                 y_copy(gap, r, g).wait_send()
+    y_low_partner().wait_send()
+    for gap in (1, 2, 3):
+        for r in range(2):
+            y_low(gap, r).wait_send()
     for i in range(2):
         half_copy(i + 1, 32 * i, i, right_x).wait_send()
     w_copy((0, 0), (0, 1), right_x).wait_send()
     w_copy((0, 0), (0, 2), left_x).wait_send()
 
     def drain(zs, _):
-        for kind in (0, 1):
+        for kind in (0, 1, 2):
             @pl.when((zs > 0) & (zs < 7))
             def _():
                 kv_copy(kind, (0, zs), (0, zs), right_z).wait_send()
@@ -594,7 +711,7 @@
         return 0
 
     lax.fori_loop(0, 8, drain, 0)
-    for kind in (0, 1):
+    for kind in (0, 1, 2):
         kv_copy(kind, (0, 7), (0, 7), right_z).wait_send()
 
 
@@ -623,13 +740,16 @@
             pltpu.VMEM((128, 1024), BF),
             pltpu.VMEM((4, 8, 256, 128), BF),
             pltpu.VMEM((4, 8, 128, 256), BF),
-            pltpu.VMEM((8, 4, 64, 1024), BF),
+            pltpu.VMEM((4, 8, LOW, 1024), BF),
+            pltpu.VMEM((8, 4, 64 - LOW, 1024), BF),
             pltpu.VMEM((1, 1024), F32),
             pltpu.VMEM((1, 1024), F32),
             pltpu.VMEM((128, 1024), F32),
             pltpu.VMEM((1024, 256), BF),
-            pltpu.VMEM((4, 2, 8, 64, 128), BF),
-            pltpu.VMEM((4, 2, 8, 64, 128), BF),
+            pltpu.VMEM((4, 2, 8, 64 - LOW, 128), BF),
+            pltpu.VMEM((4, 2, 8, 64 - LOW, 128), BF),
+            pltpu.VMEM((4, 2, 8, LOW, 128), BF),
+            pltpu.VMEM((4, 2, 8, LOW, 128), BF),
             pltpu.VMEM((1024, 128), F32),
             pltpu.VMEM((16, 2048), BF),
             pltpu.VMEM((136, 2048), F32),
@@ -642,15 +762,16 @@
             pltpu.SMEM((32, 128), F32),
             by_token, by_token, by_token,
             pltpu.VMEM((256, 128), F32),
-            states,
-            pltpu.VMEM((16, 128), F32),
-            states, states, states, states,
+            pltpu.VMEM((16, 2, 16, 128), BF),
+            pltpu.VMEM((16, 2, 16, 128), BF),
+            states, states,
             pltpu.VMEM((2, 16, 128), F32),
             pltpu.VMEM((3, 2, 16, 128), F32),
-            states, states,
-            dma((15,)), dma((4,)), dma((4,)), dma((2, 4, 8)), dma((2, 4, 8)), dma((8, 4)), dma((8, 4)),
-            dma((2,)), dma((2,)), dma((4, 2, 5)), dma((4, 2, 5)), dma((1,)), dma((1,)),
-            dma((2, 4)), dma((2, 4)), dma((2, 16)), dma((2, 16)), dma((4,)), dma((4,)),
+            pltpu.VMEM((16, 16, 128), BF),
+            pltpu.VMEM((16, 16, 128), BF),
+            dma((16,)), dma((4,)), dma((4,)), dma((3, 4, 8)), dma((3, 4, 8)), dma((8, 4)), dma((8, 4)),
+            dma((2,)), dma((2,)), dma((4, 2, 6)), dma((4, 2, 6)), dma((1,)), dma((1,)),
+            dma((2, 4)), dma((2, 4)), dma((16,)), dma((16,)), dma((4,)), dma((4,)),
             dma((16,)), dma((16,)),
         ],
         compiler_params=pltpu.CompilerParams(

time: 102 us -> 85.5 us (0.84)
  the two profiles are of different devices: /device:TPU:7 before, /device:TPU:1 now
where the time goes in v3:
time: 85.5 us; the launch traced here: 85.4 us
  Pallas kernels  82.2 us (96%)
  local copies, waits for them, and re-layouts  2.63 us (3%)
    pallas_call x1, Pallas kernels, block(): pl.pallas_call(block_kernel, out_shape=(jax.ShapeDtypeStruct(x_stream.sha...  82.2 us
    unnamed x4, local copies, waits for them, and re-layouts  2.63 us

profile of v3, /device:TPU:1, one launch (start us, length us, event | category | flops | bytes accessed | tf_op | source)
XLA Modules:
  0.0 85.4 jit_solution(16832336758821616516)
XLA Ops:
  0.6 82.2 %shard_map.158 = (bf16[128,2048]{1,0:T(8,128)(2,1)}, bf16[128,1024]{1,0:T(8,128)(2,1)}) custom-call(bf16[128,2048]{1,0:T(8,128)(2,1)} %x_hbm.1, bf16[128,2048]{1,0:T(8,128)(2,1)} %z_hbm.1, f32[4,2048]{1,0:T(4,128)} %ck_hbm.1, f32[1,2048]{1,0:T(1,128)} %bitcast.5, bf16[2048,256]{1,0:T(8,128)(2,1)} %dd_hbm.1, bf16[32,2048]{1,0:T(8,128)(2,1)} %sp_hbm.1, ...), custom_call_target="tpu_custom_call" | custom-call | tf_op jit(solution)/shard_map/pallas_call | solution.py:730
  82.8 0.0 copy-start
  82.8 1.9 %copy.19 = bf16[128,2048]{1,0:T(8,128)(2,1)} copy(bf16[128,2048]{1,0:T(8,128)(2,1)} %get-tuple-element.4) | data formatting | bytes 1048576
  84.7 0.0 copy-done
  84.7 0.7 copy.20
Async XLA Ops:
  82.8 1.9 %copy-start = (bf16[128,1024]{1,0:T(8,128)(2,1)S(1)}, bf16[128,1024]{1,0:T(8,128)(2,1)}, u32[]{:S(2)}) copy-start(bf16[128,1024]{1,0:T(8,128)(2,1)} %get-tuple-element.5) | copy-start | bytes 786436

commit v4 on v3

--- a/solution.py
+++ b/solution.py
@@ -435,6 +435,10 @@
         def _():
             w_copy((2 * h, xs), (7, xs), left_z).start()
 
+    def low_spread(zs, _):
+        spread_x(2, zs)
+        return 0
+
     def sweep(i, _):
         @pl.when(i == 1)
         def _():
@@ -460,6 +464,15 @@
             kv_arrived(kind, (2, i))
             kv_copy(kind, (near, i), (3, i), peer).start()
 
+        @pl.when(i == 6)
+        def _():
+            lax.fori_loop(0, 4, low_spread, 0)
+
+        @pl.when(i == 7)
+        def _():
+            low_hop(4)
+            lax.fori_loop(4, 8, low_spread, 0)
+
         @pl.when(i >= 2)
         def _():
             w_event(i - 2 + i // 7)
@@ -504,13 +517,6 @@
         kv_arrived(kind, (3, 7))
     attend_earlier(0, 3, 7)
 
-    low_hop(4)
-
-    def low_spread(zs, _):
-        spread_x(2, zs)
-        return 0
-
-    lax.fori_loop(0, 8, low_spread, 0)
     inverse = 1.0 / l_ref[...]
     heads = []
     for h in range(4):
@@ -630,15 +636,20 @@
     att_swap.wait()
     project(0)
     project(1)
+    w_event(8)
+    lax.fori_loop(0, 2, low_cross, 0)
     project(2)
-    w_event(8)
     w_event(9)
-    lax.fori_loop(0, 4, low_cross, 0)
+    lax.fori_loop(2, 4, low_cross, 0)
+    w_event(10)
     second_pass(0)
-    w_event(10)
     w_event(11)
+    project(3)
+    project_low()
+    for xs in range(4):
+        w_arrived((7, xs))
+    project(4)
     second_pass(1)
-    project(3)
     loads["z"].wait()
     loads["sg"].wait()
     for j in range(16):
@@ -646,13 +657,37 @@
         gate = z_ref[:, cols].astype(F32)
         mixed = scanned[pl.ds(j, 128, stride=16), :] + sg_ref[:, cols] * act[:, cols].astype(F32)
         mix_ref[:, cols] = (mixed * (gate / (1.0 + jnp.exp(-gate)))).astype(BF)
-    project_low()
-    for xs in range(4):
-        w_arrived((7, xs))
-    project(4)
-
+
+    for i in range(2):
+        half_copy(i + 1, 32 * i, i, right_x).wait_send()
+    w_copy((0, 0), (0, 1), right_x).wait_send()
+    w_copy((0, 0), (0, 2), left_x).wait_send()
+
+    def drain(zs, _):
+        for kind in (0, 1, 2):
+            @pl.when((zs > 0) & (zs < 7))
+            def _():
+                kv_copy(kind, (0, zs), (0, zs), right_z).wait_send()
+
+            for xs in range(1, 4):
+                kv_copy(kind, (xs, zs), (xs, zs), right_z).wait_send()
+
+        @pl.when(zs > 0)
+        def _():
+            for xs in range(4):
+                w_copy((zs, xs), (zs, xs), right_z).wait_send()
+
+        return 0
+
+    lax.fori_loop(0, 8, drain, 0)
+    for kind in (0, 1, 2):
+        kv_copy(kind, (0, 7), (0, 7), right_z).wait_send()
     loads["res"].wait()
     for g in range(5):
+        y_copy_partner(g).wait_send()
+        for gap in (1, 2, 3):
+            for r in range(2):
+                y_copy(gap, r, g).wait_send()
         y_arrival(0, other, g).wait_recv()
         for gap in (1, 3, 2):
             for c in range(2):
@@ -665,6 +700,10 @@
                     part = part + landed[gap, c, zs].astype(F32)
                 rows = pl.ds(pl.multiple_of(z_of(zs) * 128 + c * 64 + LOW, LOW), 64 - LOW)
                 out_t[rows, :] = part
+    y_low_partner().wait_send()
+    for gap in (1, 2, 3):
+        for r in range(2):
+            y_low(gap, r).wait_send()
     y_low_arrival(0, other).wait_recv()
     for gap in (1, 3, 2):
         for c in range(2):
@@ -679,40 +718,6 @@
     for zo in range(8):
         cols = slice(zo * 128, (zo + 1) * 128)
         out_ref[:, cols] = (res_ref[:, cols].astype(F32) + out_t[cols, :].T).astype(BF)
-
-    for g in range(5):
-        y_copy_partner(g).wait_send()
-        for gap in (1, 2, 3):
-            for r in range(2):
-                y_copy(gap, r, g).wait_send()
-    y_low_partner().wait_send()
-    for gap in (1, 2, 3):
-        for r in range(2):
-            y_low(gap, r).wait_send()
-    for i in range(2):
-        half_copy(i + 1, 32 * i, i, right_x).wait_send()
-    w_copy((0, 0), (0, 1), right_x).wait_send()
-    w_copy((0, 0), (0, 2), left_x).wait_send()
-
-    def drain(zs, _):
-        for kind in (0, 1, 2):
-            @pl.when((zs > 0) & (zs < 7))
-            def _():
-                kv_copy(kind, (0, zs), (0, zs), right_z).wait_send()
-
-            for xs in range(1, 4):
-                kv_copy(kind, (xs, zs), (xs, zs), right_z).wait_send()
-
-        @pl.when(zs > 0)
-        def _():
-            for xs in range(4):
-                w_copy((zs, xs), (zs, xs), right_z).wait_send()
-
-        return 0
-
-    lax.fori_loop(0, 8, drain, 0)
-    for kind in (0, 1, 2):
-        kv_copy(kind, (0, 7), (0, 7), right_z).wait_send()
 
 
 def block(

time: 85.5 us -> 82.3 us (0.963)
  Pallas kernels: 82.2 us -> 78.9 us
    pallas_call x1, Pallas kernels: 82.2 us -> 78.9 us  [block(): pl.pallas_call(block_kernel, out_shape=(jax.ShapeDtypeStruct(x_stream.sha...]
where the time goes in v4:
time: 82.3 us; the launch traced here: 82.2 us
  Pallas kernels  78.9 us (96%)
  local copies, waits for them, and re-layouts  2.63 us (3%)
    pallas_call x1, Pallas kernels, block(): pl.pallas_call(block_kernel, out_shape=(jax.ShapeDtypeStruct(x_stream.sha...  78.9 us
    unnamed x4, local copies, waits for them, and re-layouts  2.63 us

profile of v4, /device:TPU:1, one launch (start us, length us, event | category | flops | bytes accessed | tf_op | source)
XLA Modules:
  0.0 82.2 jit_solution(6872394481820873854)
XLA Ops:
  0.6 78.9 %shard_map.158 = (bf16[128,2048]{1,0:T(8,128)(2,1)}, bf16[128,1024]{1,0:T(8,128)(2,1)}) custom-call(bf16[128,2048]{1,0:T(8,128)(2,1)} %x_hbm.1, bf16[128,2048]{1,0:T(8,128)(2,1)} %z_hbm.1, f32[4,2048]{1,0:T(4,128)} %ck_hbm.1, f32[1,2048]{1,0:T(1,128)} %bitcast.5, bf16[2048,256]{1,0:T(8,128)(2,1)} %dd_hbm.1, bf16[32,2048]{1,0:T(8,128)(2,1)} %sp_hbm.1, ...), custom_call_target="tpu_custom_call" | custom-call | tf_op jit(solution)/shard_map/pallas_call | solution.py:735
  79.6 0.0 copy-start
  79.6 1.9 %copy.19 = bf16[128,2048]{1,0:T(8,128)(2,1)} copy(bf16[128,2048]{1,0:T(8,128)(2,1)} %get-tuple-element.4) | data formatting | bytes 1048576
  81.5 0.0 copy-done
  81.5 0.7 copy.20
Async XLA Ops:
  79.6 1.9 %copy-start = (bf16[128,1024]{1,0:T(8,128)(2,1)S(1)}, bf16[128,1024]{1,0:T(8,128)(2,1)}, u32[]{:S(2)}) copy-start(bf16[128,1024]{1,0:T(8,128)(2,1)} %get-tuple-element.5) | copy-start | bytes 786436

commit v5 on v4

--- a/solution.py
+++ b/solution.py
@@ -69,14 +69,10 @@
     def greet(peer):
         pl.semaphore_signal(barrier, inc=1, device_id=peer, device_id_type=MESH)
 
-    greet(after)
-    greet(earlier)
+    for peer in (partner, after, earlier, right_z, left_z, right_x, left_x):
+        greet(peer)
     for gap in (1, 2, 3):
-        greet(x_peer(gap))
-        for r in range(2):
-            greet(at(chip * 2 + r, (y + gap) % 4))
-    for gap in range(1, 16):
-        greet(col_peer(gap))
+        greet(at(me, (y + gap) % 4))
 
     loads = {}
     pairs = (
@@ -121,7 +117,7 @@
     loads["k"].wait()
     loads["w"].wait()
     loads["wl"].wait()
-    pl.semaphore_wait(barrier, 26)
+    pl.semaphore_wait(barrier, 10)
 
     own_rows = pl.ds(pl.multiple_of(core * 128, 128), 128)
     other_rows = pl.ds(pl.multiple_of(other * 128, 128), 128)
@@ -494,6 +490,9 @@
         @pl.when(i == 2)
         def _():
             first_pass(1)
+
+        @pl.when(i == 3)
+        def _():
             ends_stage()
 
         @pl.when(i > 0)

time: 82.3 us -> 80.9 us (0.983)
  Pallas kernels: 78.9 us -> 77.5 us
    pallas_call x1, Pallas kernels: 78.9 us -> 77.5 us  [block(): pl.pallas_call(block_kernel, out_shape=(jax.ShapeDtypeStruct(x_stream.sha...]
where the time goes in v5:
time: 80.9 us; the launch traced here: 80.8 us
  Pallas kernels  77.5 us (96%)
  local copies, waits for them, and re-layouts  2.63 us (3%)
    pallas_call x1, Pallas kernels, block(): pl.pallas_call(block_kernel, out_shape=(jax.ShapeDtypeStruct(x_stream.sha...  77.5 us
    unnamed x4, local copies, waits for them, and re-layouts  2.63 us

profile of v5, /device:TPU:1, one launch (start us, length us, event | category | flops | bytes accessed | tf_op | source)
XLA Modules:
  0.0 80.8 jit_solution(4218060228707019265)
XLA Ops:
  0.6 77.5 %shard_map.158 = (bf16[128,2048]{1,0:T(8,128)(2,1)}, bf16[128,1024]{1,0:T(8,128)(2,1)}) custom-call(bf16[128,2048]{1,0:T(8,128)(2,1)} %x_hbm.1, bf16[128,2048]{1,0:T(8,128)(2,1)} %z_hbm.1, f32[4,2048]{1,0:T(4,128)} %ck_hbm.1, f32[1,2048]{1,0:T(1,128)} %bitcast.5, bf16[2048,256]{1,0:T(8,128)(2,1)} %dd_hbm.1, bf16[32,2048]{1,0:T(8,128)(2,1)} %sp_hbm.1, ...), custom_call_target="tpu_custom_call" | custom-call | tf_op jit(solution)/shard_map/pallas_call | solution.py:734
  78.2 0.0 copy-start
  78.2 1.9 %copy.19 = bf16[128,2048]{1,0:T(8,128)(2,1)} copy(bf16[128,2048]{1,0:T(8,128)(2,1)} %get-tuple-element.4) | data formatting | bytes 1048576
  80.1 0.0 copy-done
  80.1 0.7 copy.20
Async XLA Ops:
  78.2 1.9 %copy-start = (bf16[128,1024]{1,0:T(8,128)(2,1)S(1)}, bf16[128,1024]{1,0:T(8,128)(2,1)}, u32[]{:S(2)}) copy-start(bf16[128,1024]{1,0:T(8,128)(2,1)} %get-tuple-element.5) | copy-start | bytes 786436
